TPU v7x, 32 devices: a whole 2x2x4 slice. The times are simulated.
32 devices in a mesh: dp: 8 (over z, x), tensor: 4 (over y, core).
Axes of the slice: x: 2, y: 2, z: 4, core: 2. Of those that a mesh axis runs over, the one named last changes fastest.
Arguments:
- tokens: bfloat16 [16384, 1024], P(('dp', 'tensor')), may hold values from -6 to 6
- cotangent: bfloat16 [16384, 1024], P(('dp', 'tensor')), may hold values from -6 to 6
- attention_gain: float32 [1024], replicated, may hold values from 0.5 to 1.5
- feedforward_gain: float32 [1024], replicated, may hold values from 0.5 to 1.5
- query_key_value_matrix: bfloat16 [3, 1024, 1024], P(None, 'dp', 'tensor'), may hold values from -0.1875 to 0.1875
- output_matrix: bfloat16 [1024, 1024], P('tensor', 'dp'), may hold values from -0.5 to 0.5
- feedforward_matrix: bfloat16 [2, 1024, 2816], P(None, 'dp', 'tensor'), may hold values from -0.1875 to 0.1875
- down_matrix: bfloat16 [2816, 1024], P('tensor', 'dp'), may hold values from -0.109375 to 0.109375
- memory_retention: float32 [8], replicated, may hold values from 0.3 to 0.98
- memory_step_size: float32 [8], replicated, may hold values from 0.2 to 0.9
- sequence_length: int32 [24], replicated, may hold values from 64 to 1920, as said below
- sequence_permutation: int32 [24], replicated, may hold values from 0 to 23, as said below
- sequence_adapter: int32 [24], replicated, may hold values from 0 to 7
- head_span_window: int32 [8], replicated, may hold values from 256 to 1024, as said below
- query_key_value_lower: bfloat16 [3, 1024, 128], P(None, ('dp', 'tensor')), may hold values from -0.1875 to 0.1875
- query_key_value_upper: bfloat16 [3, 128, 1024], P(None, None, ('dp', 'tensor')), may hold values from -0.75 to 0.75
- output_adapter_lower: bfloat16 [1024, 128], P(('dp', 'tensor')), may hold values from -0.1875 to 0.1875
- output_adapter_upper: bfloat16 [128, 1024], P(None, ('dp', 'tensor')), may hold values from -0.75 to 0.75
- feedforward_adapter_lower: bfloat16 [2, 1024, 128], P(None, ('dp', 'tensor')), may hold values from -0.1875 to 0.1875
- feedforward_adapter_upper: bfloat16 [2, 128, 2816], P(None, None, ('dp', 'tensor')), may hold values from -0.75 to 0.75
- down_adapter_lower: bfloat16 [2816, 128], P(('dp', 'tensor')), may hold values from -0.109375 to 0.109375
- down_adapter_upper: bfloat16 [128, 1024], P(None, ('dp', 'tensor')), may hold values from -0.75 to 0.75
Outputs:
- mixed: bfloat16 [16384, 1024], P(('dp', 'tensor'))
- token_grad: bfloat16 [16384, 1024], P(('dp', 'tensor'))
- qkv_lora_a_grad: float32 [3, 1024, 128], P(None, ('dp', 'tensor'))
- qkv_lora_b_grad: float32 [3, 128, 1024], P(None, None, ('dp', 'tensor'))
- out_lora_a_grad: float32 [1024, 128], P(('dp', 'tensor'))
- out_lora_b_grad: float32 [128, 1024], P(None, ('dp', 'tensor'))
- ffn_lora_a_grad: float32 [2, 1024, 128], P(None, ('dp', 'tensor'))
- ffn_lora_b_grad: float32 [2, 128, 2816], P(None, None, ('dp', 'tensor'))
- down_lora_a_grad: float32 [2816, 128], P(('dp', 'tensor'))
- down_lora_b_grad: float32 [128, 1024], P(None, ('dp', 'tensor'))
Inputs may be any that keep to these rules, and one draw needn't show every extreme that they name: `sequence_length`: multiples of 64; the 3 sequences that sequence_permutation lists for a group sum to 2048. `sequence_permutation`: a permutation of the sequence numbers. `head_span_window`: multiples of 256.
All inputs are finite; a program needn't handle non-finite values.
Results may differ from a plain program's by a relative error of at most 0.02.
Values may be sent and summed in bfloat16 or wider, within the bound.
No kernel may reach another device: no remote copies, remote signals or barrier semaphores. Data moves between devices by JAX's collectives and lax.ppermute only.
A program may use at most 192 MiB of HBM per device.

v0:
```python
import functools

import jax
import jax.numpy as jnp
from jax import lax
from jax.experimental import pallas as pl
from jax.experimental.pallas import tpu as pltpu
from jax.sharding import PartitionSpec as P

HEAD_DIM = 128
ADAPTER_RANK = 16
STRETCH = 64
SEQ_G = 3
LANES = 128
BLOCK = 256
MEMORY_GAIN = 32.0
EPSILON = 1e-06
LOG2E = 1.4426950408889634
BF16 = jnp.bfloat16
F32 = jnp.float32
SLABS = 8


def nn(left, right):
    return jnp.dot(left, right, preferred_element_type=F32)


def nt(left, right, precision=None):
    return lax.dot_general(
        left, right, (((1,), (1,)), ((), ())), precision=precision, preferred_element_type=F32
    )


def tn(left, right):
    return lax.dot_general(left, right, (((0,), (0,)), ((), ())), preferred_element_type=F32)


def params(mebibytes):
    return pltpu.CompilerParams(
        dimension_semantics=("arbitrary",), vmem_limit_bytes=mebibytes * 1024 * 1024
    )


def cost(flops, moved):
    return pl.CostEstimate(flops=int(flops), bytes_accessed=int(moved), transcendentals=0)


def in_hbm(values):
    return [pltpu.with_memory_space_constraint(v, pltpu.HBM) for v in values]


def whole(*shape):
    return pl.BlockSpec(shape, lambda *_: (0,) * len(shape), pipeline_mode=pl.Buffered(1))


def adapter_select(meta, first_row, rows, copies):
    row = first_row + lax.broadcasted_iota(jnp.int32, (rows, 1), 0)
    adapter = jnp.where(row >= meta[1], meta[4], jnp.where(row >= meta[0], meta[3], meta[2]))
    column = lax.broadcasted_iota(jnp.int32, (rows, copies * LANES), 1)
    return (column % LANES) // ADAPTER_RANK == adapter


def keep_low(select, values):
    return jnp.where(select, values, 0.0).astype(BF16)


def qkv_kernel(meta, *refs):
    pieces, slabs, mates = refs[:4], refs[4 : 4 + SLABS], refs[4 + SLABS : 8 + SLABS]
    gain, normed, qkv, latent, weight_out, lower_out, upper_out, *refs = refs[8 + SLABS :]
    x_all, slab_all, mate_all, x_sems, slab_sems, mate_sems = refs
    step = pl.program_id(0)
    rows = x_all.shape[1]
    kept = slab_all.shape[1]
    x_copies = [
        pltpu.make_async_copy(ref, x_all.at[k], x_sems.at[k]) for k, ref in enumerate(pieces)
    ]
    slab_copies = [
        pltpu.make_async_copy(ref.at[pl.ds(0, kept)], slab_all.at[k], slab_sems.at[k])
        for k, ref in enumerate(slabs)
    ]
    mate_copies = [
        pltpu.make_async_copy(ref, mate_all.at[k], mate_sems.at[k])
        for k, ref in enumerate(mates)
    ]
    slab, share = LANES, LANES // 4
    halves = weight_out.shape[2] // LANES
    upper_at = halves * 3 * slab

    @pl.when(step == 0)
    def _():
        for copy in slab_copies + mate_copies + x_copies:
            copy.start()
        for copy in mate_copies:
            copy.wait()
        for k in range(SLABS):
            slab_copies[k].wait()
            place = meta[8] ^ k
            wide = pl.ds(pl.multiple_of(place * slab, slab), slab)
            thin = pl.ds(pl.multiple_of(place * share, share), share)
            for m in range(3):
                for half in range(halves):
                    at = (half * 3 + m) * slab
                    weight_out[m, wide, half * LANES : (half + 1) * LANES] = slab_all[
                        k, at : at + slab, :
                    ]
                upper_out[m, thin, :] = slab_all[
                    k, upper_at + m * share : upper_at + (m + 1) * share, :
                ]
                lanes = slice(m * LANES, (m + 1) * LANES)
                for mate in range(4):
                    to = pl.multiple_of(place * slab + (meta[7] ^ mate) * share, share)
                    lower_out[pl.ds(to, share), lanes] = mate_all[
                        mate, k, m * share : (m + 1) * share, :
                    ]

    for k in range(4):

        @pl.when(step == k)
        def _(k=k):
            x_copies[k].wait()

    values = x_all[step].astype(F32)
    scale = lax.rsqrt(jnp.mean(values * values, -1, keepdims=True) + EPSILON)
    low = (values * scale * gain[...]).astype(BF16)
    normed[...] = low
    select = adapter_select(meta, (meta[7] ^ step) * rows, rows, 3)
    lat = keep_low(select, nn(low, lower_out[...]))
    latent[...] = lat
    for m in range(3):
        qkv[m] = (
            nn(low, weight_out[m]) + nt(lat[:, m * LANES : (m + 1) * LANES], upper_out[m])
        ).astype(BF16)


def project_qkv(meta, pieces, gain, slabs, mates, own):
    rows, width = pieces[0].shape
    total = rows * 4
    place = lambda step, meta: (meta[7] ^ step, 0)
    return pl.pallas_call(
        qkv_kernel,
        grid_spec=pltpu.PrefetchScalarGridSpec(
            num_scalar_prefetch=1,
            grid=(4,),
            in_specs=[pl.BlockSpec(memory_space=pltpu.HBM)] * len(pieces + slabs + mates)
            + [whole(1, width)],
            out_specs=[
                pl.BlockSpec((rows, width), place),
                pl.BlockSpec((3, rows, own), lambda step, meta: (0, meta[7] ^ step, 0)),
                pl.BlockSpec((rows, 3 * LANES), place),
                whole(3, width, own),
                whole(width, 3 * LANES),
                whole(3, own, LANES),
            ],
            scratch_shapes=[
                pltpu.VMEM((4, rows, width), BF16),
                pltpu.VMEM((SLABS, slabs[0].shape[0] - mates[0].shape[1], LANES), BF16),
                pltpu.VMEM((4,) + mates[0].shape, BF16),
                pltpu.SemaphoreType.DMA((4,)),
                pltpu.SemaphoreType.DMA((SLABS,)),
                pltpu.SemaphoreType.DMA((4,)),
            ],
        ),
        out_shape=[
            pltpu.HBM((total, width), BF16),
            pltpu.HBM((3, total, own), BF16),
            pltpu.HBM((total, 3 * LANES), BF16),
            pltpu.HBM((3, width, own), BF16),
            pltpu.HBM((width, 3 * LANES), BF16),
            pltpu.HBM((3, own, LANES), BF16),
        ],
        compiler_params=params(30),
        cost_estimate=cost(2 * total * width * (3 * own + 600), 4 * total * width),
        name="project_qkv",
    )(meta, *in_hbm(pieces + slabs + mates), gain)


def span_variants(count, spans, run):
    for n, blocks in enumerate(spans):
        if n == 0:
            condition = count <= blocks
        else:
            condition = count == blocks
        pl.when(condition)(functools.partial(run, blocks * BLOCK))


def stretch_columns(low, total_stretches):
    stretch = lax.broadcasted_iota(jnp.int32, low.shape, 0) // STRETCH
    zero = jnp.zeros_like(low)
    return jnp.concatenate(
        [jnp.where(stretch == n, low, zero) for n in range(total_stretches)], 1
    )


def unit_rows(values):
    inverse = lax.rsqrt(jnp.sum(values * values, -1, keepdims=True) + EPSILON)
    return values * inverse, inverse


def attend_forward_kernel(spans, meta, rows_in, attended, log_total, qkv, sems):
    block = pl.program_id(0)
    first_row = block * BLOCK

    def copy_of(b):
        rows = pl.ds(b * BLOCK, BLOCK)
        return pltpu.make_async_copy(rows_in.at[:, rows], qkv.at[:, rows], sems.at[b])

    @pl.when(block == 0)
    def _():
        for b in range(qkv.shape[1] // BLOCK):
            copy_of(b).start()

    for b in range(qkv.shape[1] // BLOCK):

        @pl.when(block == (0 if b == 1 else b))
        def _(b=b):
            copy_of(b).wait()

    start_two, start_three = meta[0], meta[1]
    row = first_row + lax.broadcasted_iota(jnp.int32, (BLOCK, 1), 0)
    begin = jnp.where(row >= start_three, start_three, jnp.where(row >= start_two, start_two, 0))
    first_begin = jnp.where(
        first_row >= start_three, start_three, jnp.where(first_row >= start_two, start_two, 0)
    )
    factor = HEAD_DIM ** (-0.5) * LOG2E
    here = pl.ds(pl.multiple_of(first_row, BLOCK), BLOCK)
    windows = meta[5], meta[6]
    low_keys = [jnp.maximum(row - window + 1, begin) for window in windows]
    first_key = jnp.maximum(first_row - jnp.maximum(*windows) + 1, first_begin)

    def attend(span):
        start = pl.multiple_of(jnp.maximum(first_row + BLOCK - span, 0), BLOCK)
        there = pl.ds(start, span)
        position = start + lax.broadcasted_iota(jnp.int32, (BLOCK, span), 1)
        heads = [slice(h * HEAD_DIM, (h + 1) * HEAD_DIM) for h in range(2)]
        scores = [nt(qkv[0, here, cols], qkv[1, there, cols]) for cols in heads]
        for h, cols in enumerate(heads):
            allowed = (position >= low_keys[h]) & (position <= row)
            score = jnp.where(allowed, scores[h], -1e30)
            top = jnp.max(score, -1, keepdims=True)
            weight = jnp.exp2((score - top) * factor).astype(BF16)
            value = qkv[2, there, cols]
            both = nn(weight, jnp.concatenate([value, jnp.ones_like(value)], 1))
            total = both[:, HEAD_DIM : HEAD_DIM + 1]
            attended[:, cols] = (both[:, :HEAD_DIM] / both[:, HEAD_DIM:]).astype(BF16)
            logs = jnp.broadcast_to(top * factor + jnp.log2(total), (BLOCK, LANES))
            pick = jnp.where(lax.broadcasted_iota(jnp.int32, (8, LANES), 1) == 0, 1.0, 0.0)
            log_total[0, h : h + 1, :] = nt(pick, logs, lax.Precision.HIGHEST)[0:1]

    span_variants(block - first_key // BLOCK + 1, spans, attend)


def attend_forward(meta, qkv, spans):
    total, own = qkv.shape[1:]
    blocks = total // BLOCK
    return pl.pallas_call(
        functools.partial(attend_forward_kernel, spans),
        grid_spec=pltpu.PrefetchScalarGridSpec(
            num_scalar_prefetch=1,
            grid=(blocks,),
            in_specs=[pl.BlockSpec(memory_space=pltpu.HBM)],
            out_specs=[
                pl.BlockSpec((BLOCK, own), lambda b, *_: (b, 0)),
                pl.BlockSpec((1, 8, BLOCK), lambda b, *_: (b, 0, 0)),
            ],
            scratch_shapes=[
                pltpu.VMEM(qkv.shape, BF16),
                pltpu.SemaphoreType.DMA((blocks,)),
            ],
        ),
        out_shape=[
            jax.ShapeDtypeStruct((total, own), BF16),
            jax.ShapeDtypeStruct((blocks, 8, BLOCK), F32),
        ],
        compiler_params=params(18),
        cost_estimate=cost(4e9, 12e6),
        name="attend_forward",
    )(meta, *in_hbm([qkv]))


def memory_forward_kernel(meta, fmeta, qkv, attended, near, far, states, heads, state_scr):
    block = pl.program_id(0)
    first_row = block * BLOCK
    start_two, start_three = meta[0], meta[1]
    stretches = BLOCK // STRETCH

    @pl.when(block == 0)
    def _():
        state_scr[...] = jnp.zeros_like(state_scr)

    columns = [slice(h * HEAD_DIM, (h + 1) * HEAD_DIM) for h in range(2)]
    queries, grams, writtens = [], [], []
    for h, cols in enumerate(columns):
        query_unit, _ = unit_rows(qkv[0, :, cols].astype(F32))
        key_unit, _ = unit_rows(qkv[1, :, cols].astype(F32))
        by_stretch = stretch_columns(key_unit.astype(BF16), stretches)
        step_size = fmeta[2 + h]
        queries.append(query_unit.astype(BF16))
        grams.append((nn(key_unit.T.astype(BF16), by_stretch) * step_size).astype(BF16))
        turned = qkv[2, :, cols].astype(F32).T.astype(BF16)
        writtens.append(nn(turned, by_stretch) * step_size)
    carried = [state_scr[h] for h in range(2)]
    for n in range(stretches):
        row_at = first_row + n * STRETCH
        keep = jnp.where((row_at == start_two) | (row_at == start_three), 0.0, 1.0)
        lanes = slice(n * HEAD_DIM, (n + 1) * HEAD_DIM)
        for h in range(2):
            state = carried[h] * keep
            low = state.astype(BF16)
            states[n, h] = low
            carried[h] = fmeta[h] * state - nn(low, grams[h][:, lanes]) + writtens[h][:, lanes]
    for h, cols in enumerate(columns):
        state_scr[h] = carried[h]
        for n in range(stretches):
            rows = slice(n * STRETCH, (n + 1) * STRETCH)
            read = nt(queries[h][rows], states[n, h])
            heads[rows, cols] = (attended[rows, cols].astype(F32) + MEMORY_GAIN * read).astype(BF16)

    half_blocks = near.shape[0] // BLOCK
    at = pl.ds(pl.multiple_of((block % half_blocks) * BLOCK, BLOCK), BLOCK)
    own_chip = block // half_blocks == meta[7] // 2

    @pl.when(own_chip)
    def _():
        near[at, :] = heads[...]

    @pl.when(jnp.logical_not(own_chip))
    def _():
        far[at, :] = heads[...]


def memory_forward(meta, fmeta, qkv, attended):
    total, own = qkv.shape[1:]
    blocks = total // BLOCK
    stretches = BLOCK // STRETCH
    return pl.pallas_call(
        memory_forward_kernel,
        grid_spec=pltpu.PrefetchScalarGridSpec(
            num_scalar_prefetch=2,
            grid=(blocks,),
            in_specs=[
                pl.BlockSpec((3, BLOCK, own), lambda b, *_: (0, b, 0)),
                pl.BlockSpec((BLOCK, own), lambda b, *_: (b, 0)),
            ],
            out_specs=[
                whole(total // 2, own),
                whole(total // 2, own),
                pl.BlockSpec(
                    (stretches, 2, HEAD_DIM, HEAD_DIM), lambda b, *_: (b, 0, 0, 0)
                ),
            ],
            scratch_shapes=[
                pltpu.VMEM((BLOCK, own), BF16),
                pltpu.VMEM((2, HEAD_DIM, HEAD_DIM), F32),
            ],
        ),
        out_shape=[
            jax.ShapeDtypeStruct((total // 2, own), BF16),
            jax.ShapeDtypeStruct((total // 2, own), BF16),
            pltpu.HBM((blocks * stretches, 2, HEAD_DIM, HEAD_DIM), BF16),
        ],
        compiler_params=params(10),
        cost_estimate=cost(1e5, 1e5),
        name="memory_forward",
    )(meta, fmeta, *in_hbm([qkv, attended]))


def mixer_backward_kernel(
    spans,
    blocks,
    meta,
    fmeta,
    qkv,
    grad_near,
    grad_far,
    attended,
    log_total,
    states,
    grads,
    grad_out,
    key_t,
    key_sum,
    value_sum,
    query_t,
    state_grad,
):
    block = blocks - 1 - pl.program_id(0)
    first_row = block * BLOCK
    start_two, start_three = meta[0], meta[1]
    row = first_row + lax.broadcasted_iota(jnp.int32, (1, BLOCK), 1)
    begin = jnp.where(row >= start_three, start_three, jnp.where(row >= start_two, start_two, 0))
    first_begin = jnp.where(
        first_row >= start_three, start_three, jnp.where(first_row >= start_two, start_two, 0)
    )
    scale = HEAD_DIM ** (-0.5)
    factor = scale * LOG2E
    stretches = BLOCK // STRETCH
    here = pl.ds(pl.multiple_of(first_row, BLOCK), BLOCK)
    per_piece = grad_near.shape[0] // 2 // BLOCK
    piece = (block // per_piece) ^ meta[7]
    at = pl.ds(
        pl.multiple_of(((piece % 2) * per_piece + block % per_piece) * BLOCK, BLOCK), BLOCK
    )

    @pl.when(piece < 2)
    def _():
        grad_out[...] = grad_near[at, :]

    @pl.when(piece >= 2)
    def _():
        grad_out[...] = grad_far[at, :]

    @pl.when(pl.program_id(0) == 0)
    def _():
        key_sum[...] = jnp.zeros_like(key_sum)
        value_sum[...] = jnp.zeros_like(value_sum)
        state_grad[...] = jnp.zeros_like(state_grad)
        for h in range(2):
            for b in range(blocks):
                rows = slice(b * BLOCK, (b + 1) * BLOCK)
                key = qkv[1, rows, h * HEAD_DIM : (h + 1) * HEAD_DIM]
                key_t[h, :, rows] = key.astype(F32).T.astype(BF16)

    windows = meta[5], meta[6]
    low_keys = [jnp.maximum(row - window + 1, begin) for window in windows]
    first_key = jnp.maximum(first_row - jnp.maximum(*windows) + 1, first_begin)
    heads = [slice(h * HEAD_DIM, (h + 1) * HEAD_DIM) for h in range(2)]
    ones = jnp.ones((8, HEAD_DIM), F32)
    inners = [
        nt(ones, grad_out[:, cols].astype(F32) * attended[:, cols].astype(F32), lax.Precision.HIGHEST)[0:1]
        for cols in heads
    ]

    def attend(span):
        start = pl.multiple_of(jnp.maximum(first_row + BLOCK - span, 0), BLOCK)
        there = pl.ds(start, span)
        position = start + lax.broadcasted_iota(jnp.int32, (span, BLOCK), 0)
        scores = [nt(qkv[1, there, cols], qkv[0, here, cols]) for cols in heads]
        grad_weights = [nt(qkv[2, there, cols], grad_out[:, cols]) for cols in heads]
        for h, cols in enumerate(heads):
            allowed = (position >= low_keys[h]) & (position <= row)
            weight = jnp.where(
                allowed, jnp.exp2(scores[h] * factor - log_total[0, h : h + 1, :]), 0.0
            )
            grad_score = (weight * (grad_weights[h] - inners[h])).astype(BF16)
            value_sum[h, there, :] += nn(weight.astype(BF16), grad_out[:, cols])
            key_sum[h, there, :] += nn(grad_score, qkv[0, here, cols])
            query_t[h] = nn(key_t[h, :, there], grad_score)

    def remember():
        for h in range(2):
            cols = slice(h * HEAD_DIM, (h + 1) * HEAD_DIM)
            query_unit, query_inverse = unit_rows(qkv[0, here, cols].astype(F32))
            key_unit, key_inverse = unit_rows(qkv[1, here, cols].astype(F32))
            value = qkv[2, here, cols].astype(F32)
            key_low = key_unit.astype(BF16)
            grad = grad_out[:, cols]
            retention, step_size = fmeta[h], fmeta[2 + h]
            gram = (
                nn(key_unit.T.astype(BF16), stretch_columns(key_low, stretches)) * step_size
            ).astype(BF16)
            read_grad = MEMORY_GAIN * nn(
                grad.astype(F32).T.astype(BF16),
                stretch_columns(query_unit.astype(BF16), stretches),
            )
            carried = state_grad[h]
            query_grads, key_grads, value_grads = [], [], []
            for n in reversed(range(stretches)):
                row_at = first_row + n * STRETCH
                keep = jnp.where((row_at == start_two) | (row_at == start_three), 0.0, 1.0)
                rows = slice(n * STRETCH, (n + 1) * STRETCH)
                lanes = slice(n * HEAD_DIM, (n + 1) * HEAD_DIM)
                carried_low = carried.astype(BF16)
                state = states[n, h]
                key_rows = key_low[rows]
                pulled = nt(key_rows, carried_low)
                error = nt(key_rows, state) - value[rows]
                value_grads.append(step_size * pulled)
                key_grads.append(
                    -step_size
                    * (nn(pulled.astype(BF16), state) + nn(error.astype(BF16), carried_low))
                )
                query_grads.append(MEMORY_GAIN * nn(grad[rows], state))
                carried = keep * (
                    read_grad[:, lanes] + retention * carried - nn(carried_low, gram[:, lanes])
                )
            state_grad[h] = carried
            query_unit_grad = jnp.concatenate(query_grads[::-1], 0)
            key_unit_grad = jnp.concatenate(key_grads[::-1], 0)
            value_grad = jnp.concatenate(value_grads[::-1], 0)
            query_memory = query_inverse * (
                query_unit_grad
                - query_unit * jnp.sum(query_unit * query_unit_grad, -1, keepdims=True)
            )
            key_memory = key_inverse * (
                key_unit_grad - key_unit * jnp.sum(key_unit * key_unit_grad, -1, keepdims=True)
            )
            grads[0, :, cols] = (scale * query_t[h].T + query_memory).astype(BF16)
            grads[1, :, cols] = (scale * key_sum[h, here, :] + key_memory).astype(BF16)
            grads[2, :, cols] = (value_sum[h, here, :] + value_grad).astype(BF16)

    def both(span):
        attend(span)
        remember()

    span_variants(block - first_key // BLOCK + 1, spans, both)


def mixer_backward(meta, fmeta, qkv, grad_near, grad_far, attended, log_total, states, spans):
    total, own = qkv.shape[1:]
    blocks = total // BLOCK
    stretches = BLOCK // STRETCH
    row_block = pl.BlockSpec((BLOCK, own), lambda s, *_: (blocks - 1 - s, 0))
    return pl.pallas_call(
        functools.partial(mixer_backward_kernel, spans, blocks),
        grid_spec=pltpu.PrefetchScalarGridSpec(
            num_scalar_prefetch=2,
            grid=(blocks,),
            in_specs=[
                whole(*qkv.shape),
                whole(*grad_near.shape),
                whole(*grad_far.shape),
                row_block,
                pl.BlockSpec((1, 8, BLOCK), lambda s, *_: (blocks - 1 - s, 0, 0)),
                pl.BlockSpec(
                    (stretches, 2, HEAD_DIM, HEAD_DIM), lambda s, *_: (blocks - 1 - s, 0, 0, 0)
                ),
            ],
            out_specs=pl.BlockSpec((3, BLOCK, own), lambda s, *_: (0, blocks - 1 - s, 0)),
            scratch_shapes=[
                pltpu.VMEM((BLOCK, own), BF16),
                pltpu.VMEM((2, HEAD_DIM, total), BF16),
                pltpu.VMEM((2, total, HEAD_DIM), F32),
                pltpu.VMEM((2, total, HEAD_DIM), F32),
                pltpu.VMEM((2, HEAD_DIM, BLOCK), F32),
                pltpu.VMEM((2, HEAD_DIM, HEAD_DIM), F32),
            ],
        ),
        out_shape=jax.ShapeDtypeStruct(qkv.shape, BF16),
        compiler_params=params(20),
        cost_estimate=cost(10e9, 16e6),
        name="mixer_backward",
    )(meta, fmeta, qkv, grad_near, grad_far, attended, log_total, states)


def unpack_kernel(meta, pack, f0, f1, f2, f3, used, wide, down, out, lower, out_upper, down_upper, out_lower):
    hidden = down.shape[0]
    width = out.shape[1]
    heads = out.shape[0] // 2
    share = LANES // 4
    first_out, first_lower = 3 * hidden, 3 * hidden + 2 * heads
    skip = f0.shape[1] - 4 * share
    for p in range(SLABS):
        lanes = slice(p * LANES, (p + 1) * LANES)
        wide[:, lanes] = pack[p, : 2 * hidden, :]
        down[:, lanes] = pack[p, 2 * hidden : 3 * hidden, :]
        out[:, lanes] = pack[p, first_out : first_out + 2 * heads, :]
        for n in range(2):
            at = first_lower + n * share
            to = n * heads + p * share
            out_lower[to : to + share, :] = pack[p, at : at + share, :]
        for k, ref in enumerate((f0, f1, f2, f3)):
            place = (meta[8] ^ p) * LANES + (meta[7] ^ k) * share
            to = pl.ds(pl.multiple_of(place, share), share)
            part = lambda n, ref=ref: ref[p, skip + n * share : skip + (n + 1) * share, :]
            lower[to, :LANES] = part(0)
            lower[to, LANES:] = part(1)
            out_upper[to, :] = part(2)
            down_upper[to, :] = part(3)
    wide[:hidden, width:] = used[0]
    wide[hidden:, width:] = used[1]
    down[:, width:] = used[2]


def unpack(meta, pack, fulls, used, hidden, heads):
    width = SLABS * LANES
    shapes = [
        (2 * hidden, width + LANES),
        (hidden, width + LANES),
        (2 * heads, width),
        (width, 2 * LANES),
        (width, LANES),
        (width, LANES),
        (2 * heads, LANES),
    ]
    return pl.pallas_call(
        unpack_kernel,
        grid_spec=pltpu.PrefetchScalarGridSpec(
            num_scalar_prefetch=1,
            grid=(1,),
            in_specs=[whole(*v.shape) for v in (pack, *fulls, used)],
            out_specs=[whole(*v) for v in shapes],
        ),
        out_shape=[jax.ShapeDtypeStruct(v, BF16) for v in shapes],
        compiler_params=params(20),
        cost_estimate=cost(1e5, 1e5),
        name="unpack",
    )(meta, pack, *fulls, used)


def out_forward_kernel(meta, near, far, weight, lower, upper_t, own, mate, latent, heads):
    rows, columns = own.shape[0], near.shape[1]
    for k, out in enumerate((own, mate)):
        at = pl.ds(pl.multiple_of(((meta[7] % 2) ^ k) * rows, rows), rows)
        both = jnp.concatenate([near[at, :], far[at, :]], 1)
        here = slice(k * rows, (k + 1) * rows)
        heads[here, :] = both
        select = adapter_select(meta, (meta[7] ^ k) * rows, rows, 1)
        lat = keep_low(select, nn(both, lower[...]))
        latent[here, :] = lat
        out[...] = (nn(both, weight[...]) + nt(lat, upper_t[...])).astype(BF16)


def out_forward(meta, near, far, weight, lower, upper_t):
    rows, columns = near.shape[0] // 2, near.shape[1]
    width = upper_t.shape[0]
    return pl.pallas_call(
        out_forward_kernel,
        grid_spec=pltpu.PrefetchScalarGridSpec(
            num_scalar_prefetch=1,
            grid=(1,),
            in_specs=[whole(*v.shape) for v in (near, far, weight, lower, upper_t)],
            out_specs=[
                whole(rows, width),
                whole(rows, width),
                whole(2 * rows, LANES),
                whole(2 * rows, 2 * columns),
            ],
        ),
        out_shape=[
            jax.ShapeDtypeStruct((rows, width), BF16),
            jax.ShapeDtypeStruct((rows, width), BF16),
            jax.ShapeDtypeStruct((2 * rows, LANES), BF16),
            jax.ShapeDtypeStruct((2 * rows, 2 * columns), BF16),
        ],
        compiler_params=params(14),
        cost_estimate=cost(1e5, 1e5),
        name="out_forward",
    )(meta, near, far, weight, lower, upper_t)


def out_backward_kernel(meta, grad_own, grad_mate, weight, lower, upper_t, mine, other, latent):
    rows, columns = grad_own.shape[0], mine.shape[1]
    for k, grad in enumerate((grad_own, grad_mate)):
        here = slice(k * rows, (k + 1) * rows)
        select = adapter_select(meta, (meta[7] ^ k) * rows, rows, 1)
        lat = keep_low(select, nn(grad[...], upper_t[...]))
        latent[here, :] = lat
        both = (nt(grad[...], weight[...]) + nt(lat, lower[...])).astype(BF16)
        mine[here, :] = both[:, :columns]
        other[here, :] = both[:, columns:]


def out_backward(meta, grad_own, grad_mate, weight, lower, upper_t):
    rows, width = grad_own.shape
    columns = lower.shape[0] // 2
    return pl.pallas_call(
        out_backward_kernel,
        grid_spec=pltpu.PrefetchScalarGridSpec(
            num_scalar_prefetch=1,
            grid=(1,),
            in_specs=[whole(*v.shape) for v in (grad_own, grad_mate, weight, lower, upper_t)],
            out_specs=[
                whole(2 * rows, columns),
                whole(2 * rows, columns),
                whole(2 * rows, LANES),
            ],
        ),
        out_shape=[
            jax.ShapeDtypeStruct((2 * rows, columns), BF16),
            jax.ShapeDtypeStruct((2 * rows, columns), BF16),
            jax.ShapeDtypeStruct((2 * rows, LANES), BF16),
        ],
        compiler_params=params(14),
        cost_estimate=cost(4 * rows * width * 640, 8e6),
        name="out_backward",
    )(meta, grad_own, grad_mate, weight, lower, upper_t)


def spread_shares(meta, turned, out, lanes):
    share = LANES // 4
    for mate in range(4):
        for p in range(SLABS):
            at = pl.multiple_of(p * LANES + (meta[7] ^ mate) * share, share)
            out[mate, p * share : (p + 1) * share, lanes] = turned[pl.ds(at, share), :]


def out_pairs_kernel(meta, heads, latent_grad, latent, grad_own, grad_mate, lower_out, upper_out, turned):
    rows = grad_own.shape[0]
    lower_out[...] = tn(latent_grad[...], heads[...]).T.astype(BF16)
    turned[...] = (
        (tn(latent[:rows], grad_own[...]) + tn(latent[rows:], grad_mate[...])).T
    ).astype(BF16)
    spread_shares(meta, turned, upper_out, slice(None))


def out_pairs(meta, heads, latent_grad, latent, grad_own, grad_mate):
    rows, width = grad_own.shape
    columns = heads.shape[1]
    return pl.pallas_call(
        out_pairs_kernel,
        grid_spec=pltpu.PrefetchScalarGridSpec(
            num_scalar_prefetch=1,
            grid=(1,),
            in_specs=[whole(*v.shape) for v in (heads, latent_grad, latent, grad_own, grad_mate)],
            out_specs=[whole(columns, LANES), whole(4, width // 4, LANES)],
            scratch_shapes=[pltpu.VMEM((width, LANES), BF16)],
        ),
        out_shape=[
            jax.ShapeDtypeStruct((columns, LANES), BF16),
            jax.ShapeDtypeStruct((4, width // 4, LANES), BF16),
        ],
        compiler_params=params(12),
        cost_estimate=cost(4 * rows * LANES * (columns + width), 5e6),
        name="out_pairs",
    )(meta, heads, latent_grad, latent, grad_own, grad_mate)


def ffn_kernel(
    first,
    meta,
    x0,
    x1,
    g0,
    g1,
    weight,
    down_weight,
    lower,
    down_upper_t,
    dx0,
    dx1,
    swiglu,
    pre_grads,
    latent,
    latent_grad,
    down_latent_grad,
):
    step = pl.program_id(0)
    rows = swiglu.shape[0]
    parts = x0.shape[0] // rows
    width, hidden = x0.shape[1], swiglu.shape[1]

    for k, (x_ref, g_ref, dx_ref) in enumerate(((x0, g0, dx0), (x1, g1, dx1))):

        @pl.when(step // parts == k)
        def _(k=k, x_ref=x_ref, g_ref=g_ref, dx_ref=dx_ref):
            part = step % parts
            at = pl.ds(pl.multiple_of(part * rows, rows), rows)
            first_row = (meta[7] ^ (first + k)) * (rows * parts) + part * rows
            select = adapter_select(meta, first_row, rows, 2)
            x = x_ref[at, :]
            grad = g_ref[at, :]
            lat = keep_low(select, nn(x, lower[...]))
            latent[...] = lat
            gate = nt(jnp.concatenate([x, lat[:, :LANES]], 1), weight[:hidden])
            up = nt(jnp.concatenate([x, lat[:, LANES:]], 1), weight[hidden:])
            down_lat = keep_low(select[:, :LANES], nn(grad, down_upper_t[...]))
            down_latent_grad[...] = down_lat
            wide_grad = nt(jnp.concatenate([grad, down_lat], 1), down_weight[...])
            sigmoid = 1.0 / (1.0 + jnp.exp(-gate))
            silu = gate * sigmoid
            swiglu[...] = (silu * up).astype(BF16)
            d_up = (wide_grad * silu).astype(BF16)
            d_gate = (wide_grad * up * (sigmoid * (1.0 + gate * (1.0 - sigmoid)))).astype(BF16)
            pre_grads[0] = d_gate
            pre_grads[1] = d_up
            lat_grad = keep_low(
                select,
                jnp.concatenate(
                    [nn(d_gate, weight[:hidden, width:]), nn(d_up, weight[hidden:, width:])], 1
                ),
            )
            latent_grad[...] = lat_grad
            dx_ref[at, :] = (
                nn(d_gate, weight[:hidden, :width])
                + nn(d_up, weight[hidden:, :width])
                + nt(lat_grad, lower[...])
            ).astype(BF16)


def ffn(meta, first, xs, grads, weight, down_weight, lower, down_upper_t):
    rows, width = xs[0].shape
    hidden = down_weight.shape[0]
    total = 2 * rows
    block = lambda columns: pl.BlockSpec((BLOCK, columns), lambda s, *_: (s, 0))
    return pl.pallas_call(
        functools.partial(ffn_kernel, first),
        grid_spec=pltpu.PrefetchScalarGridSpec(
            num_scalar_prefetch=1,
            grid=(total // BLOCK,),
            in_specs=[
                whole(*v.shape)
                for v in (*xs, *grads, weight, down_weight, lower, down_upper_t)
            ],
            out_specs=[whole(rows, width)] * 2
            + [
                block(hidden),
                pl.BlockSpec((2, BLOCK, hidden), lambda s, *_: (0, s, 0)),
                block(2 * LANES),
                block(2 * LANES),
                block(LANES),
            ],
        ),
        out_shape=[jax.ShapeDtypeStruct((rows, width), BF16)] * 2
        + [
            pltpu.HBM((total, hidden), BF16),
            pltpu.HBM((2, total, hidden), BF16),
            jax.ShapeDtypeStruct((total, 2 * LANES), BF16),
            jax.ShapeDtypeStruct((total, 2 * LANES), BF16),
            jax.ShapeDtypeStruct((total, LANES), BF16),
        ],
        compiler_params=params(28),
        cost_estimate=cost(2 * total * width * hidden * 6.0, 14e6),
        name="ffn",
    )(meta, *xs, *grads, weight, down_weight, lower, down_upper_t)


def ffn_rest_kernel(steps, meta, *refs):
    xs, grads, refs = refs[:4], refs[4:8], refs[8:]
    near, far, refs = refs[:5], refs[5:10], refs[10:]
    weight, upper_t = refs[:2]
    branches, refs = refs[2:6], refs[6:]
    sums_out, x_sum, gate_sum, up_sum, down_sum, branch_sum, turned = refs
    step = pl.program_id(0)
    hidden, rows = weight.shape[0], xs[0].shape[0]
    width = xs[0].shape[1]

    @pl.when(step == 0)
    def _():
        for total in (x_sum, gate_sum, up_sum, down_sum, branch_sum):
            total[...] = jnp.zeros_like(total)

    for k in range(4):

        @pl.when(step == k)
        def _(k=k):
            swiglu, pre_grads, latent, latent_grad, down_latent_grad = near if k < 2 else far
            wide = swiglu[...]
            select = adapter_select(meta, (meta[7] ^ k) * rows, rows, 1)
            lat = keep_low(select, nn(wide, weight[:, width:]))
            branches[k][...] = (nn(wide, weight[:, :width]) + nt(lat, upper_t[...])).astype(BF16)
            x_sum[...] += tn(latent_grad[...], xs[k][...])
            gate_sum[:, :hidden] += tn(latent[:, :LANES], pre_grads[0])
            up_sum[:, :hidden] += tn(latent[:, LANES:], pre_grads[1])
            down_sum[:, :hidden] += tn(down_latent_grad[...], wide)
            branch_sum[...] += tn(lat, grads[k][...])

    @pl.when(step == steps - 1)
    def _():
        turned[:, : 2 * LANES] = x_sum[...].T
        turned[:, 2 * LANES :] = branch_sum[...].T
        share, used = LANES // 4, hidden // SLABS
        for p in range(SLABS):
            for mate in range(4):
                at = pl.multiple_of(p * LANES + (meta[7] ^ mate) * share, share)
                for n in range(3):
                    to = (mate * 3 + n) * share
                    sums_out[p, to : to + share, :] = turned[
                        pl.ds(at, share), n * LANES : (n + 1) * LANES
                    ]
        for n, total in enumerate((gate_sum, up_sum, down_sum)):
            values = total[...].T
            for p in range(SLABS):
                to = 12 * share + n * used
                sums_out[p, to : to + used, :] = values[p * used : (p + 1) * used]


def ffn_rest(meta, xs, grads, near, far, weight, upper_t):
    rows, width = xs[0].shape
    hidden = weight.shape[0]
    padded = -(-hidden // LANES) * LANES
    operands = (*xs, *grads, *near, *far, weight, upper_t)

    def kept(values, first):
        step_of = lambda s: jnp.clip(s - first, 0, 1)
        if values.ndim == 3:
            return pl.BlockSpec((2, rows, hidden), lambda s, *_: (0, step_of(s), 0))
        return pl.BlockSpec((rows, values.shape[1]), lambda s, *_: (step_of(s), 0))

    return pl.pallas_call(
        functools.partial(ffn_rest_kernel, 4),
        grid_spec=pltpu.PrefetchScalarGridSpec(
            num_scalar_prefetch=1,
            grid=(4,),
            in_specs=[whole(*v.shape) for v in (*xs, *grads)]
            + [kept(v, 0) for v in near]
            + [kept(v, 2) for v in far]
            + [whole(*v.shape) for v in (weight, upper_t)],
            out_specs=[whole(rows, width)] * 4
            + [whole(SLABS, 3 * LANES + 3 * hidden // SLABS, LANES)],
            scratch_shapes=[
                pltpu.VMEM((2 * LANES, width), F32),
                pltpu.VMEM((LANES, padded), F32),
                pltpu.VMEM((LANES, padded), F32),
                pltpu.VMEM((LANES, padded), F32),
                pltpu.VMEM((LANES, width), F32),
                pltpu.VMEM((width, 3 * LANES), F32),
            ],
        ),
        out_shape=[jax.ShapeDtypeStruct((rows, width), BF16)] * 4
        + [jax.ShapeDtypeStruct((SLABS, 3 * LANES + 3 * hidden // SLABS, LANES), F32)],
        compiler_params=params(36),
        cost_estimate=cost(8 * rows * width * hidden * 2.3, 30e6),
        name="ffn_rest",
    )(meta, *operands)


def qkv_backward_kernel(first, meta, grads0, grads1, weight, lower, upper_t, dx0, dx1):
    rows = dx0.shape[0]
    for k, (grads, dx) in enumerate(((grads0, dx0), (grads1, dx1))):
        select = adapter_select(meta, (meta[7] ^ (first + k)) * rows, rows, 3)
        lat = keep_low(
            select, jnp.concatenate([nn(grads[m], upper_t[m]) for m in range(3)], 1)
        )
        total = nt(lat, lower[...])
        for m in range(3):
            total += nt(grads[m], weight[m])
        dx[...] = total.astype(BF16)


def qkv_backward(meta, first, rows, grads, weight, lower, upper_t):
    own = grads.shape[2]
    width = lower.shape[0]
    piece = lambda k: pl.BlockSpec((3, rows, own), lambda s, meta: (0, meta[7] ^ (first + k), 0))
    return pl.pallas_call(
        functools.partial(qkv_backward_kernel, first),
        grid_spec=pltpu.PrefetchScalarGridSpec(
            num_scalar_prefetch=1,
            grid=(1,),
            in_specs=[
                piece(0),
                piece(1),
                whole(*weight.shape),
                whole(*lower.shape),
                whole(*upper_t.shape),
            ],
            out_specs=[whole(rows, width)] * 2,
        ),
        out_shape=[jax.ShapeDtypeStruct((rows, width), BF16)] * 2,
        compiler_params=params(16),
        cost_estimate=cost(4 * rows * width * 50, 4e5),
        name="qkv_backward",
    )(meta, grads, grads, weight, lower, upper_t)


def qkv_pairs_kernel(steps, meta, normed, latent, grads, upper_t, lower_out, upper_out, low_sum, up_sum, turned):
    step = pl.program_id(0)
    rows = normed.shape[0]
    select = adapter_select(meta, step * rows, rows, 3)
    lat = keep_low(
        select, jnp.concatenate([nn(grads[m], upper_t[m]) for m in range(3)], 1)
    )

    @pl.when(step == 0)
    def _():
        low_sum[...] = jnp.zeros_like(low_sum)
        up_sum[...] = jnp.zeros_like(up_sum)

    low_sum[...] += tn(lat, normed[...])
    for m in range(3):
        up_sum[m] += tn(latent[:, m * LANES : (m + 1) * LANES], grads[m])

    @pl.when(step == steps - 1)
    def _():
        turned[...] = low_sum[...].T.astype(BF16)
        spread_shares(meta, turned, lower_out, slice(None))
        for m in range(3):
            upper_out[m] = up_sum[m].T.astype(BF16)


def qkv_pairs(meta, normed, latent, grads, upper_t):
    total, width = normed.shape
    own = grads.shape[2]
    rows = 1024
    steps = total // rows
    return pl.pallas_call(
        functools.partial(qkv_pairs_kernel, steps),
        grid_spec=pltpu.PrefetchScalarGridSpec(
            num_scalar_prefetch=1,
            grid=(steps,),
            in_specs=[
                pl.BlockSpec((rows, width), lambda s, *_: (s, 0)),
                pl.BlockSpec((rows, 3 * LANES), lambda s, *_: (s, 0)),
                pl.BlockSpec((3, rows, own), lambda s, *_: (0, s, 0)),
                whole(*upper_t.shape),
            ],
            out_specs=[whole(4, width // 4, 3 * LANES), whole(3, own, LANES)],
            scratch_shapes=[
                pltpu.VMEM((3 * LANES, width), F32),
                pltpu.VMEM((3, LANES, own), F32),
                pltpu.VMEM((width, 3 * LANES), BF16),
            ],
        ),
        out_shape=[
            jax.ShapeDtypeStruct((4, width // 4, 3 * LANES), BF16),
            jax.ShapeDtypeStruct((3, own, LANES), BF16),
        ],
        compiler_params=params(20),
        cost_estimate=cost(2 * total * width * 20, 4e5),
        name="qkv_pairs",
    )(meta, normed, latent, grads, upper_t)


def join_norm_kernel(stream, own, got, gain, hidden, normed):
    values = stream[...].astype(F32) + (own[...].astype(F32) + got[...].astype(F32))
    hidden[...] = values.astype(BF16)
    scale = lax.rsqrt(jnp.mean(values * values, -1, keepdims=True) + EPSILON)
    normed[...] = (values * scale * gain[...]).astype(BF16)


def join_norm(stream, own, got, gain):
    rows, width = stream.shape
    return pl.pallas_call(
        join_norm_kernel,
        grid=(1,),
        in_specs=[whole(*v.shape) for v in (stream, own, got, gain)],
        out_specs=[whole(rows, width)] * 2,
        out_shape=[
            jax.ShapeDtypeStruct((rows, width), BF16),
            jax.ShapeDtypeStruct((rows, width), BF16),
        ],
        compiler_params=params(12),
        cost_estimate=cost(1e5, 1e5),
        name="join_norm",
    )(stream, own, got, gain)


def norm_gradient_kernel(*refs):
    operands, (gain, out), (held, sems) = refs[:5], refs[5:7], refs[7:]
    copies = [
        pltpu.make_async_copy(ref, held.at[k], sems.at[k]) for k, ref in enumerate(operands)
    ]
    for copy in copies:
        copy.start()
    for copy in copies:
        copy.wait()
    straight, values, own, near, far = [held[k].astype(F32) for k in range(5)]
    grad = own + near + far
    inverse = lax.rsqrt(jnp.mean(values * values, -1, keepdims=True) + EPSILON)
    scaled = gain[...] * grad
    inner = jnp.mean(scaled * values, -1, keepdims=True)
    out[...] = (
        straight + (inverse * scaled - values * (inverse * inverse * inverse * inner))
    ).astype(BF16)


def norm_gradient(straight, values, own, near, far, gain, stay=False):
    rows, width = values.shape
    operands = [straight, values, own, near, far]
    operands = in_hbm(operands) if stay else operands
    place = pltpu.HBM if stay else pl.ANY
    return pl.pallas_call(
        norm_gradient_kernel,
        grid=(1,),
        in_specs=[pl.BlockSpec(memory_space=place)] * 5 + [whole(1, width)],
        out_specs=whole(rows, width),
        out_shape=jax.ShapeDtypeStruct((rows, width), BF16),
        scratch_shapes=[pltpu.VMEM((5, rows, width), BF16), pltpu.SemaphoreType.DMA((5,))],
        compiler_params=params(20),
        cost_estimate=cost(1e6, 9e6),
        name="norm_gradient",
    )(*operands, gain)


def swap(values, bit):
    size = lax.axis_size("tensor")
    return lax.ppermute(values, "tensor", [(i, i ^ bit) for i in range(size)])


def swap_dp(values, bits):
    size = lax.axis_size("dp")
    return lax.ppermute(values, "dp", [(i, i ^ bits) for i in range(size)])


def gather_tensor(values):
    far = swap(values, 2)
    return [values, swap(values, 1), far, swap(far, 1)]


def tensor_order(pieces, place):
    stacked = jnp.stack(pieces)
    for bit in (1, 2):
        moved = stacked.reshape((2, 2) + pieces[0].shape)[:, ::-1] if bit == 1 else (
            stacked.reshape((2, 2) + pieces[0].shape)[::-1]
        )
        stacked = jnp.where((place & bit) != 0, moved.reshape(stacked.shape), stacked)
    return stacked


def gather_slabs(values):
    near = [values] + [swap_dp(values, 2 * k) for k in (1, 2, 3)]
    result = []
    for piece in near:
        result += [piece, swap_dp(piece, 1)]
    return result


def pieces_dp(values):
    size = lax.axis_size("dp")
    if size != SLABS:
        exchanged = exchange_dp(values)
        return [exchanged[k] for k in range(size)]
    place = lax.axis_index("dp")
    sent = [lax.dynamic_index_in_dim(values, place ^ k, 0, keepdims=False) for k in range(size)]
    return sent[:1] + [swap_dp(sent[k], k) for k in range(1, size)]


def exchange_dp(values):
    return lax.all_to_all(values, "dp", split_axis=0, concat_axis=0, tiled=True)


def after(values, *earlier):
    return lax.optimization_barrier((values,) + earlier)[0]


def together(*values):
    return lax.optimization_barrier(values)


def per_device(
    tokens,
    cotangent,
    attention_gain,
    feedforward_gain,
    query_key_value_matrix,
    output_matrix,
    feedforward_matrix,
    down_matrix,
    memory_retention,
    memory_step_size,
    sequence_length,
    sequence_permutation,
    sequence_adapter,
    head_span_window,
    query_key_value_lower,
    query_key_value_upper,
    output_adapter_lower,
    output_adapter_upper,
    feedforward_adapter_lower,
    feedforward_adapter_upper,
    down_adapter_lower,
    down_adapter_upper,
):
    groups = lax.axis_size("dp")
    group = lax.axis_index("dp")
    place = lax.axis_index("tensor")
    quarter, width = tokens.shape
    slot = quarter // groups
    heads_own = query_key_value_matrix.shape[2]
    hidden = feedforward_matrix.shape[2]

    members = lax.dynamic_slice_in_dim(sequence_permutation, group * SEQ_G, SEQ_G)
    hits = members[:, None] == jnp.arange(sequence_length.shape[0], dtype=jnp.int32)[None, :]
    lengths = jnp.sum(jnp.where(hits, sequence_length[None, :], 0), 1)
    adapters = jnp.sum(jnp.where(hits, sequence_adapter[None, :], 0), 1)
    head_at = place * 2
    windows = lax.dynamic_slice_in_dim(head_span_window, head_at, 2)
    meta = jnp.concatenate(
        [
            jnp.stack([lengths[0], lengths[0] + lengths[1]]),
            adapters,
            windows,
            jnp.stack([place, group if groups == SLABS else jnp.zeros_like(group)]),
        ]
    ).astype(jnp.int32)
    fmeta = jnp.concatenate(
        [
            lax.dynamic_slice_in_dim(memory_retention, head_at, 2),
            lax.dynamic_slice_in_dim(memory_step_size, head_at, 2) / STRETCH,
        ]
    )
    spans = (2, 3, 4, 5)
    axes = ("dp", "tensor")
    tensors = lax.axis_size("tensor")
    to_user = [(j, (j % groups) * tensors + j // groups) for j in range(groups * tensors)]
    to_owner = [(b, a) for a, b in to_user]
    share = query_key_value_lower.shape[1]
    up_share = feedforward_adapter_upper.shape[2]
    turn = lambda values: jnp.swapaxes(values, -1, -2)

    def flat(*parts):
        return jnp.concatenate([v.reshape(-1, LANES) for v in parts], 0)

    fulls = (feedforward_adapter_lower, turn(output_adapter_upper), turn(down_adapter_upper))

    arrived = exchange_dp(tokens.reshape(groups, slot, width)).reshape(quarter, width)
    token_pieces = gather_tensor(arrived)
    if groups == SLABS:
        halves = jnp.moveaxis(
            query_key_value_matrix.reshape(3, width // groups, heads_own // LANES, LANES), 2, 0
        )
        pack = flat(
            halves,
            lax.ppermute(turn(query_key_value_upper), axes, to_user),
            query_key_value_lower,
            *fulls,
        )
        slabs = gather_slabs(after(pack, arrived))
        lower_rows = pack.shape[0] - 7 * share
        mates = gather_tensor(jnp.stack([v[lower_rows:] for v in slabs]))
    else:
        halves = lax.all_gather(query_key_value_matrix, "dp", axis=1, tiled=True)
        halves = jnp.moveaxis(halves.reshape(3, SLABS, LANES, heads_own // LANES, LANES), (1, 3), (0, 1))
        upper = lax.all_gather(lax.ppermute(turn(query_key_value_upper), axes, to_user), "dp", axis=1, tiled=True)
        upper = jnp.swapaxes(upper.reshape(3, SLABS, heads_own // SLABS, LANES), 0, 1)
        lower = lax.all_gather(query_key_value_lower, axes, axis=1, tiled=True)
        lower = jnp.moveaxis(lower.reshape(3, SLABS, 4, LANES // 4, LANES), (2, 1), (0, 1))
        lower = lower.reshape(4, SLABS, 3 * LANES // 4, LANES)
        at = lambda k: lax.dynamic_index_in_dim(lower, place ^ k, 0, keepdims=False)
        pack = jnp.concatenate(
            [v.reshape(SLABS, -1, LANES) for v in (halves, upper, at(0))], 1
        )
        slabs = [pack[k] for k in range(SLABS)]
        mates = [at(k) for k in range(4)]

    cot_arrived = exchange_dp(
        after(cotangent, mates[3]).reshape(groups, slot, width)
    ).reshape(quarter, width)
    wide = (turn(feedforward_matrix), down_matrix, output_matrix, swap(output_matrix, 2))
    out_lower_used, *users = [
        lax.ppermute(v, axes, to_user)
        for v in (output_adapter_lower, turn(feedforward_adapter_upper), down_adapter_lower)
    ]
    out_used = (out_lower_used, swap(out_lower_used, 2))
    if groups == SLABS:
        pack = after(flat(*wide, *out_used, *users), slabs[6])
        pack = lax.all_gather(pack, "dp", axis=0, tiled=False)

    gain_one = attention_gain.reshape(1, width)
    gain_two = feedforward_gain.reshape(1, width)
    normed, qkv, qkv_latent, qkv_w, qkv_a, qkv_b = project_qkv(
        meta, token_pieces, gain_one, slabs, mates, heads_own
    )
    attended, log_total = attend_forward(meta, qkv, spans)
    heads_near, heads_sent, states = memory_forward(meta, fmeta, qkv, attended)
    heads_far = swap(heads_sent, 2)
    cot_arrived = after(cot_arrived, heads_far)
    grad_mate, grad_far = swap(cot_arrived, 1), swap(cot_arrived, 2)
    grad_pieces = [cot_arrived, grad_mate, grad_far]
    if groups == SLABS:
        pack = after(pack, heads_near, cot_arrived)
        at = 3 * hidden + 2 * heads_own
        used = pack[:, at + 2 * share :].reshape(SLABS, 3, up_share, LANES)
        used = jnp.swapaxes(used, 0, 1).reshape(3, hidden, LANES)
        ffn_w, down_w, out_w, ffn_a, out_b, down_b, out_a = unpack(
            meta, pack, mates, used, hidden, heads_own
        )
    else:
        gathered = [lax.all_gather(v, "dp", axis=v.ndim - 1, tiled=True) for v in wide]
        ffn_a, out_b, down_b = [
            lax.all_gather(v, axes, axis=v.ndim - 2, tiled=True) for v in fulls
        ]
        ffn_a = jnp.concatenate([ffn_a[0], ffn_a[1]], 1)
        ffn_b, down_a, *out_a = [
            lax.all_gather(v, "dp", axis=v.ndim - 2, tiled=True) for v in (*users, *out_used)
        ]
        out_a = jnp.concatenate(out_a, 0)
        ffn_w = jnp.concatenate([gathered[0], ffn_b], 2).reshape(2 * hidden, width + LANES)
        down_w = jnp.concatenate([gathered[1], down_a], 1)
        out_w = jnp.concatenate(gathered[2:], 0)
    heads_far, grad_pieces[2] = together(heads_far, grad_pieces[2])
    branch_own, branch_mate, out_latent, heads = out_forward(
        meta, heads_near, heads_far, out_w, out_a, out_b
    )
    branch_got = swap(branch_mate, 1)
    hidden_one, normed_two = join_norm(arrived, branch_own, branch_got, gain_two)
    two = [normed_two, swap(normed_two, 1)]
    two_far = swap(normed_two, 2)

    two[0], grad_pieces[2] = together(two[0], grad_pieces[2])
    near = ffn(meta, 0, two, grad_pieces[:2], ffn_w, down_w, ffn_a, down_b)
    two_far = after(two_far, near[0])
    grad_pieces = grad_pieces + [swap(grad_pieces[2], 1)]
    two = two + [two_far, swap(two_far, 1)]
    far = ffn(meta, 2, two[2:], grad_pieces[2:], ffn_w, down_w, ffn_a, down_b)

    def first_step(far_mate, across):
        return (far_mate.astype(F32) + swap(across, 1).astype(F32)).astype(BF16)

    def second_step(own, mate, onward):
        return own.astype(F32) + swap(mate, 1).astype(F32) + swap(onward, 2).astype(F32)

    def scatter(own, mate, far_mate, across):
        return second_step(own, mate, first_step(far_mate, across))

    onward = first_step(far[0], far[1])
    onward, *far = together(onward, *far[2:])
    onward_far = swap(onward, 2)
    *branch, ffn_sums = ffn_rest(meta, two, grad_pieces, near[2:], far, down_w, down_b)
    onward_far, *branch = together(onward_far, *branch)
    grad_one = norm_gradient(
        cot_arrived, hidden_one, near[0], swap(near[1], 1), onward_far, gain_two
    )

    grad_mate = swap(grad_one, 1)
    head_grads, head_grads_sent, out_latent_grad = out_backward(
        meta, grad_one, grad_mate, out_w, out_a, out_b
    )
    head_grads_far = swap(head_grads_sent, 2)
    out_own, out_full = out_pairs(
        meta, heads, after(out_latent_grad, head_grads_sent), out_latent, grad_one, grad_mate
    )
    def reduce_pack(full_terms, own_terms):
        parts = scatter(*[full_terms[k] for k in range(4)]).astype(BF16)
        parts = parts.reshape(groups, share, full_terms.shape[2])
        parts = [
            parts[:, :, i * LANES : (i + 1) * LANES]
            for i in range(full_terms.shape[2] // LANES)
        ]
        return jnp.concatenate(parts + own_terms, 1)

    def reduced(exchanged, parts):
        summed = sum(v.astype(F32) for v in exchanged)
        cut = share * parts
        own = lax.ppermute(summed[cut:], axes, to_owner)
        return summed[:cut].reshape(parts, share, LANES), own

    def by_owner(values):
        return values.reshape(groups, values.shape[0] // groups, LANES)

    def regroup(values):
        if groups == SLABS:
            return values
        rows = values.reshape(4, SLABS, LANES // 4, values.shape[2])
        ordered = tensor_order([rows[k] for k in range(4)], place)
        ordered = jnp.swapaxes(ordered, 0, 1).reshape(groups, tensors, share, values.shape[2])
        at = lambda k: lax.dynamic_index_in_dim(ordered, place ^ k, 1, keepdims=False)
        return jnp.stack([at(k).reshape(groups * share, values.shape[2]) for k in range(4)])

    def by_dp(sums):
        if groups == SLABS:
            return sums
        parts = sums[:, : 3 * LANES].reshape(SLABS, 4, 3, LANES // 4, LANES)
        parts = tensor_order([parts[:, k] for k in range(4)], place)
        parts = jnp.moveaxis(parts, (1, 0, 3), (0, 1, 2)).reshape(groups, tensors, share, 3, LANES)
        at = lambda k: lax.dynamic_index_in_dim(parts, place ^ k, 1, keepdims=False)
        parts = [jnp.swapaxes(at(k), 1, 2).reshape(groups, -1, LANES) for k in range(4)]
        own = sums[:, 3 * LANES :].reshape(SLABS, 3, hidden // SLABS, LANES)
        own = jnp.swapaxes(own, 0, 1).reshape(3, groups, up_share, LANES)
        return jnp.concatenate(parts + [own[n] for n in range(3)], 1)

    ffn_sums = lax.psum_scatter(by_dp(ffn_sums), "dp", scatter_dimension=0, tiled=False)
    branch_onward = first_step(branch[2], branch[3])
    head_grads_far, branch_onward, out_own, out_full = together(
        head_grads_far, branch_onward, out_own, out_full
    )
    branch_far = swap(branch_onward, 2)
    branch_near = branch[0].astype(F32) + swap(branch[1], 1).astype(F32)
    qkv_grads = mixer_backward(
        meta, fmeta, qkv, head_grads, head_grads_far, attended, log_total, states, spans
    )
    qkv_grads, branch_far = together(qkv_grads, branch_far)

    far_terms = qkv_backward(meta, 2, quarter, qkv_grads, qkv_w, qkv_a, qkv_b)
    onward = first_step(*far_terms)
    branch_far = after(branch_far, far_terms[0])
    mixed_rows = (hidden_one.astype(F32) + (branch_near + branch_far.astype(F32))).astype(BF16)
    mixed_rows = after(mixed_rows, onward)
    mixed = exchange_dp(mixed_rows.reshape(groups, slot, width)).reshape(quarter, width)
    qkv_grads = after(qkv_grads, onward)
    onward_far = swap(onward, 2)
    near_terms = qkv_backward(meta, 0, quarter, qkv_grads, qkv_w, qkv_a, qkv_b)
    near_got = swap(near_terms[1], 1)
    qkv_full, qkv_own = qkv_pairs(
        meta, normed, qkv_latent, after(qkv_grads, near_terms[0]), qkv_b
    )
    onward_far, mixed = together(onward_far, mixed)
    grad_input = norm_gradient(
        grad_one, arrived, near_terms[0], near_got, onward_far, gain_one, True
    )
    token_grad = exchange_dp(grad_input.reshape(groups, slot, width)).reshape(quarter, width)
    qkv_full, qkv_own, out_own, out_full, _ = together(
        qkv_full, qkv_own, out_own, out_full, onward_far
    )
    out_mine, out_other = by_owner(out_own[:heads_own]), by_owner(out_own[heads_own:])
    out_mine = (out_mine.astype(F32) + swap(out_other, 2).astype(F32)).astype(BF16)
    qkv_pack = reduce_pack(
        regroup(jnp.concatenate([qkv_full, out_full], 2)),
        [by_owner(qkv_own[m]) for m in range(3)] + [out_mine],
    )
    qkv_full, qkv_own = reduced(pieces_dp(qkv_pack), 4)
    ffn_sums = after(ffn_sums, grad_input)
    ffn_parts = [ffn_sums[k * 3 * share : (k + 1) * 3 * share] for k in range(4)]
    ffn_onward = ffn_parts[2] + swap(ffn_parts[3], 1)
    ffn_full = ffn_parts[0] + swap(ffn_parts[1], 1) + swap(ffn_onward, 2)
    ffn_full = ffn_full.reshape(3, share, LANES)
    ffn_own = lax.ppermute(ffn_sums[12 * share :], axes, to_owner)
    ffn_own_parts = [ffn_own[i * up_share : (i + 1) * up_share] for i in range(3)]
    return (
        mixed,
        token_grad,
        qkv_full[:3],
        turn(qkv_own[: 3 * share].reshape(3, share, LANES)),
        qkv_own[3 * share :],
        qkv_full[3].T,
        ffn_full[:2],
        jnp.stack([ffn_own_parts[0].T, ffn_own_parts[1].T]),
        ffn_own_parts[2],
        ffn_full[2].T,
    )


def solution(mesh):
    both = ("dp", "tensor")
    rows = P(both, None)
    lower = P(None, both, None)
    upper = P(None, None, both)
    return jax.shard_map(
        per_device,
        mesh=mesh,
        in_specs=(
            rows,
            rows,
            P(),
            P(),
            P(None, "dp", "tensor"),
            P("tensor", "dp"),
            P(None, "dp", "tensor"),
            P("tensor", "dp"),
            P(),
            P(),
            P(),
            P(),
            P(),
            P(),
            lower,
            upper,
            rows,
            P(None, both),
            lower,
            upper,
            rows,
            P(None, both),
        ),
        out_specs=(
            rows,
            rows,
            lower,
            upper,
            rows,
            P(None, both),
            lower,
            upper,
            rows,
            P(None, both),
        ),
        check_vma=False,
    )
```

profile of v0, /device:TPU:2, one launch (start us, length us, event | category | flops | bytes accessed | tf_op | source)
XLA Modules:
  0.0 457.4 jit_solution(1163677965758892515)
XLA Ops:
  7.3 6.5 %all-to-all-start = ((bf16[8,64,1024]{2,1,0:T(8,128)(2,1)}), bf16[8,64,1024]{2,1,0:T(8,128)(2,1)S(1)}, u32[]{:S(2)}, u32[]{:S(2)}) async-start(bf16[8,64,1024]{2,1,0:T(8,128)(2,1)} %bitcast.145), calls=%async_computation | async-start | bytes 2097152 | tf_op jit(solution)/shard_map/all_to_all | solution.py:1108
  13.9 4.3 collective-permute-start.3
  18.1 2.4 collective-permute-start.16
  20.6 1.9 collective-permute-start.17
  22.5 2.5 collective-permute-start.19
  25.0 3.4 collective-permute-start.20
  28.6 3.3 collective-permute-done.17
  32.0 9.9 %collective-permute-start.18 = (bf16[32,128]{1,0:T(8,128)(2,1)S(1)}, bf16[32,128]{1,0:T(8,128)(2,1)S(1)}, u32[]{:S(2)}, u32[]{:S(2)}) collective-permute-start(bf16[32,128]{1,0:T(8,128)(2,1)S(1)} %collective-permute-done.17), channel_id=1, source_target_pairs={{0,2},{1,3},{2,0},{3,1},{4,6},{5,7},{6,4},{7,5},{8,10},{9,11},{10,... | collective-permute-start | bytes 24584 | tf_op jit(solution)/shard_map/ppermute | solution.py:1066
  43.7 7.5 %collective-permute-done.9.refs_10_ = bf16[1088,128]{1,0:T(8,128)(2,1)S(1)} collective-permute-done((bf16[1088,128]{1,0:T(8,128)(2,1)S(1)}, bf16[1088,128]{1,0:T(8,128)(2,1)S(1)}, u32[]{:S(2)}, u32[]{:S(2)}) %collective-permute-start.9) | collective-permute-done | bytes 278560 | tf_op jit(solution)/shard_map/ppermute | solution.py:1071
  51.2 5.6 %collective-permute-start.5 = (bf16[1088,128]{1,0:T(8,128)(2,1)S(1)}, bf16[1088,128]{1,0:T(8,128)(2,1)S(1)}, u32[]{:S(2)}, u32[]{:S(2)}) collective-permute-start(bf16[1088,128]{1,0:T(8,128)(2,1)S(1)} %constant_dynamic-update-slice_fusion.refs_4_), channel_id=1, source_target_pairs={{0,8},{4,12},{8,0},{12,4},{16,24},{20,28},{24,16},{28,20},{1,9},{5... | collective-permute-start | bytes 835592 | tf_op jit(solution)/shard_map/ppermute | solution.py:1071
  57.7 2.0 collective-permute-start.4
  60.6 13.3 %collective-permute-done.5.refs_6_ = bf16[1088,128]{1,0:T(8,128)(2,1)S(1)} collective-permute-done((bf16[1088,128]{1,0:T(8,128)(2,1)S(1)}, bf16[1088,128]{1,0:T(8,128)(2,1)S(1)}, u32[]{:S(2)}, u32[]{:S(2)}) %collective-permute-start.5) | collective-permute-done | bytes 278560 | tf_op jit(solution)/shard_map/ppermute | solution.py:1071
  73.9 2.9 collective-permute-start.6
  76.9 10.4 %collective-permute-done.6.refs_7_ = bf16[1088,128]{1,0:T(8,128)(2,1)S(1)} collective-permute-done((bf16[1088,128]{1,0:T(8,128)(2,1)S(1)}, bf16[1088,128]{1,0:T(8,128)(2,1)S(1)}, u32[]{:S(2)}, u32[]{:S(2)}) %collective-permute-start.6) | collective-permute-done | bytes 278560 | tf_op jit(solution)/shard_map/ppermute | solution.py:1071
  87.4 4.8 %collective-permute-done.8.refs_9_ = bf16[1088,128]{1,0:T(8,128)(2,1)S(1)} collective-permute-done((bf16[1088,128]{1,0:T(8,128)(2,1)S(1)}, bf16[1088,128]{1,0:T(8,128)(2,1)S(1)}, u32[]{:S(2)}, u32[]{:S(2)}) %collective-permute-start.8) | collective-permute-done | bytes 278560 | tf_op jit(solution)/shard_map/ppermute | solution.py:1071
  93.8 10.0 %collective-permute-done.12.refs_14_.f2 = bf16[8,224,128]{2,1,0:T(8,128)(2,1)S(1)} collective-permute-done((bf16[8,224,128]{2,1,0:T(8,128)(2,1)S(1)}, bf16[8,224,128]{2,1,0:T(8,128)(2,1)S(1)}, u32[]{:S(2)}, u32[]{:S(2)}) %collective-permute-start.12) | collective-permute-done | bytes 458784 | tf_op jit(solution)/shard_map/ppermute | solution.py:1066
  106.4 4.5 all-to-all-start.1
  114.0 14.4 %project_qkv.1 = (bf16[2048,1024]{1,0:T(8,128)(2,1)}, bf16[3,2048,256]{2,1,0:T(8,128)(2,1)}, bf16[2048,384]{1,0:T(8,128)(2,1)}, bf16[3,1024,256]{2,1,0:T(8,128)(...) custom-call(s32[9]{0:T(128)S(1)} %concatenate.18.meta, bf16[512,1024]{1,0:T(8,128)(2,1)} %bitcast.127, ...), custom_call_target="tpu_custom_call" | custom-call | flops 5737807872 | bytes 8388608 | tf_op jit(solution)/shard_map/project_qkv/pallas_call | solution.py:139
  128.4 15.4 %attend_forward.1 = (bf16[2048,256]{1,0:T(8,128)(2,1)S(1)}, f32[8,8,256]{2,1,0:T(8,128)S(1)}) custom-call(s32[9]{0:T(128)S(1)} %concatenate.18.meta, bf16[3,2048,256]{2,1,0:T(8,128)(2,1)} %get-tuple-element.104.rows_in.qkv), custom_call_target="tpu_custom_call" | custom-call | flops 4000000000 | bytes 12000000 | tf_op jit(solution)/shard_map/attend_forward/pallas_call | solution.py:255
  144.7 11.5 %memory_forward.1 = (bf16[1024,256]{1,0:T(8,128)(2,1)S(1)}, bf16[1024,256]{1,0:T(8,128)(2,1)S(1)}, bf16[32,2,128,128]{3,2,1,0:T(8,128)(2,1)}) custom-call(s32[9]{0:T(128)S(1)} %concatenate.18.meta, f32[4]{0:T(128)S(1)} %pad_maximum_fusion.1.fmeta, bf16[3,2048,256]{2,1,0:T(8,128)(2,1)} %get-tuple-element.104.rows_in.qkv, bf16[2048,256]{1,0:T(8,128)(2,1)} %copy-done.16), custom_call_target="tpu_custom_call" | custom-call | flops 100000 | bytes 100000 | tf_op jit(solution)/shard_map/memory_forward/pallas_call | solution.py:335
  156.3 1.9 collective-permute-start.14
  158.2 12.9 %collective-permute-done.14.far = bf16[1024,256]{1,0:T(8,128)(2,1)S(1)} collective-permute-done((bf16[1024,256]{1,0:T(8,128)(2,1)S(1)}, bf16[1024,256]{1,0:T(8,128)(2,1)S(1)}, u32[]{:S(2)}, u32[]{:S(2)}) %collective-permute-start.14) | collective-permute-done | bytes 524320 | tf_op jit(solution)/shard_map/ppermute | solution.py:1066
  171.4 25.0 %collective-permute-done.15.g0.refs_6_ = bf16[512,1024]{1,0:T(8,128)(2,1)} collective-permute-done((bf16[512,1024]{1,0:T(8,128)(2,1)S(1)}, bf16[512,1024]{1,0:T(8,128)(2,1)}, u32[]{:S(2)}, u32[]{:S(2)}) %collective-permute-start.15) | collective-permute-done | bytes 1048608 | tf_op jit(solution)/shard_map/ppermute | solution.py:1066
  197.6 2.7 copy-done.5
  201.3 2.8 unpack.1
  204.2 2.9 out_forward.1
  208.6 2.1 collective-permute-done.21.got
  212.2 2.0 collective-permute-done.22.x1.refs_1_
  214.2 15.2 %ffn.2 = (bf16[512,1024]{1,0:T(8,128)(2,1)S(1)}, bf16[512,1024]{1,0:T(8,128)(2,1)S(1)}, bf16[1024,704]{1,0:T(8,128)(2,1)}, bf16[2,1024,704]{2,1,0:T(8,128)(2,1)}...) custom-call(s32[9]{0:T(128)S(1)} %concatenate.18.meta, ...), custom_call_target="tpu_custom_call" | custom-call | flops 8858370048 | bytes 14000000 | tf_op jit(solution)/shard_map/ffn/pallas_call | solution.py:785
  229.4 7.7 %collective-permute-done.25.x0.refs_2_ = bf16[512,1024]{1,0:T(8,128)(2,1)S(1)} collective-permute-done((bf16[512,1024]{1,0:T(8,128)(2,1)S(1)}, bf16[512,1024]{1,0:T(8,128)(2,1)S(1)}, u32[]{:S(2)}, u32[]{:S(2)}) %collective-permute-start.25) | collective-permute-done | bytes 1048608 | tf_op jit(solution)/shard_map/ppermute | solution.py:1066
  237.1 2.7 collective-permute-done.26.x1.refs_3_
  239.8 16.8 %ffn.3 = (bf16[512,1024]{1,0:T(8,128)(2,1)S(1)}, bf16[512,1024]{1,0:T(8,128)(2,1)S(1)}, bf16[1024,704]{1,0:T(8,128)(2,1)}, bf16[2,1024,704]{2,1,0:T(8,128)(2,1)}...) custom-call(s32[9]{0:T(128)S(1)} %concatenate.18.meta, ...), custom_call_target="tpu_custom_call" | custom-call | flops 8858370048 | bytes 14000000 | tf_op jit(solution)/shard_map/ffn/pallas_call | solution.py:785
  257.9 2.5 collective-permute-done.28
  261.2 15.9 %ffn_rest.1 = (bf16[512,1024]{1,0:T(8,128)(2,1)S(1)}, bf16[512,1024]{1,0:T(8,128)(2,1)S(1)}, bf16[512,1024]{1,0:T(8,128)(2,1)S(1)}, bf16[512,1024]{1,0:T(8,128)(2,1)}, f32[8,648,128]{2,1,0:T(8,128)}) custom-call(s32[9]{0:T(128)S(1)} %concatenate.18.meta, bf16[512,1024]{1,0:T(8,128)(2,1)S(1)} %get-tuple-element.121.x0.refs_0_, ...), custom_call_target="tpu_custom_call" | custom-call | flops 6791416832 | bytes 30000000 | tf_op jit(solution)/shard_map/ffn_rest/pallas_call | solution.py:879
  277.1 9.0 %collective-permute-done.29.refs_4_ = bf16[512,1024]{1,0:T(8,128)(2,1)S(1)} collective-permute-done((bf16[512,1024]{1,0:T(8,128)(2,1)S(1)}, bf16[512,1024]{1,0:T(8,128)(2,1)S(1)}, u32[]{:S(2)}, u32[]{:S(2)}) %collective-permute-start.29) | collective-permute-done | bytes 1048608 | tf_op jit(solution)/shard_map/ppermute | solution.py:1066
  286.1 1.6 norm_gradient.2.grad_own.refs_0_
  288.3 2.9 collective-permute-done.30.grad_mate
  292.2 3.8 out_backward.1
  296.5 2.7 out_pairs.1
  299.9 1.8 add_convert_fusion.2
  301.7 8.4 %collective-permute-done.31.grad_far = bf16[1024,256]{1,0:T(8,128)(2,1)S(1)} collective-permute-done((bf16[1024,256]{1,0:T(8,128)(2,1)S(1)}, bf16[1024,256]{1,0:T(8,128)(2,1)S(1)}, u32[]{:S(2)}, u32[]{:S(2)}) %collective-permute-start.31) | collective-permute-done | bytes 524320 | tf_op jit(solution)/shard_map/ppermute | solution.py:1066
  310.5 28.5 %mixer_backward.1.grads0.grads1.grads = bf16[3,2048,256]{2,1,0:T(8,128)(2,1)S(1)} custom-call(s32[9]{0:T(128)S(1)} %concatenate.18.meta, f32[4]{0:T(128)S(1)} %pad_maximum_fusion.1.fmeta, bf16[3,2048,256]{2,1,0:T(8,128)(2,1)S(1)} %copy-done.13, bf16[1024,256]{1,0:T(8,128)(2,1)S(1)} %get-tuple-element.153.grad_near, ...), custom_call_target="tpu_custom_call" | custom-call | flops 10000000000 | bytes 16000000 | tf_op jit(solution)/shard_map/mixer_backward/pallas_call | solution.py:513
  339.1 3.8 qkv_backward.2
  342.9 1.8 collective-permute-start.34
  344.7 1.9 add_convert_fusion
  348.4 5.2 %all-to-all-start.2 = ((bf16[8,64,1024]{2,1,0:T(8,128)(2,1)}), bf16[8,64,1024]{2,1,0:T(8,128)(2,1)}, u32[]{:S(2)}, u32[]{:S(2)}) async-start(bf16[8,64,1024]{2,1,0:T(8,128)(2,1)} %bitcast.142), calls=%async_computation.2 | async-start | bytes 2097152 | tf_op jit(solution)/shard_map/all_to_all | solution.py:1108
  356.4 4.8 %qkv_backward.3 = (bf16[512,1024]{1,0:T(8,128)(2,1)S(1)}, bf16[512,1024]{1,0:T(8,128)(2,1)}) custom-call(s32[9]{0:T(128)S(1)} %concatenate.18.meta, bf16[3,2048,256]{2,1,0:T(8,128)(2,1)S(1)} %mixer_backward.1.grads0.grads1.grads, bf16[3,2048,256]{2,1,0:T(8,128)(2,1)S(1)} %mixer_backward.1.grads0.grads1.grads, bf16[3,1024,256]{2,1,0:T(8,128)(2,1)S(1)} %copy-done.7, ...), custom_call_target="tpu_custom_call" | custom-call | flops 104857600 | bytes 400000 | tf_op jit(solution)/shard_map/qkv_backward/pallas_call | solution.py:924
  362.3 2.2 copy-done.8
  365.9 5.1 %qkv_pairs.1 = (bf16[4,256,384]{2,1,0:T(8,128)(2,1)S(1)}, bf16[3,256,128]{2,1,0:T(8,128)(2,1)S(1)}) custom-call(s32[9]{0:T(128)S(1)} %concatenate.18.meta, bf16[2048,1024]{1,0:T(8,128)(2,1)S(1)} %copy-done.8, bf16[2048,384]{1,0:T(8,128)(2,1)S(1)} %copy-done.15, bf16[3,2048,256]{2,1,0:T(8,128)(2,1)S(1)} %mixer_backward.1.grads0.grads1.grads, ...), custom_call_target="tpu_custom_call" | custom-call | flops 83886080 | bytes 400000 | tf_op jit(solution)/shard_map/qkv_pairs/pallas_call | solution.py:975
  372.6 6.1 %collective-permute-done.35.refs_4_ = bf16[512,1024]{1,0:T(8,128)(2,1)} collective-permute-done((bf16[512,1024]{1,0:T(8,128)(2,1)}, bf16[512,1024]{1,0:T(8,128)(2,1)}, u32[]{:S(2)}, u32[]{:S(2)}) %collective-permute-start.35) | collective-permute-done | bytes 1048608 | tf_op jit(solution)/shard_map/ppermute | solution.py:1066
  379.9 4.7 %norm_gradient.3 = bf16[512,1024]{1,0:T(8,128)(2,1)} custom-call(bf16[512,1024]{1,0:T(8,128)(2,1)} %copy-done.4, bf16[512,1024]{1,0:T(8,128)(2,1)} %bitcast.128, bf16[512,1024]{1,0:T(8,128)(2,1)} %copy-done.24, bf16[512,1024]{1,0:T(8,128)(2,1)} %collective-permute-done.37.refs_3_, bf16[512,1024]{1,0:T(8,128)(2,1)} %collective-permute-done.35.refs_4_, ...), custom_call_target="tpu_custom_call" | custom-call | flops 1000000 | bytes 9000000 | tf_op jit(solution)/shard_map/norm_gradient/pallas_call | solution.py:1051
  386.4 4.9 %all-to-all-start.3 = ((bf16[8,64,1024]{2,1,0:T(8,128)(2,1)}), bf16[8,64,1024]{2,1,0:T(8,128)(2,1)S(1)}, u32[]{:S(2)}, u32[]{:S(2)}) async-start(bf16[8,64,1024]{2,1,0:T(8,128)(2,1)} %bitcast.34), calls=%async_computation.3 | async-start | bytes 2097152 | tf_op jit(solution)/shard_map/all_to_all | solution.py:1108
  393.6 1.9 collective-permute-start.53
  396.4 3.8 collective-permute-start.52
  400.3 2.1 collective-permute-done.52
  404.5 4.8 %collective-permute-done.40 = bf16[256,512]{1,0:T(8,128)(2,1)S(1)} collective-permute-done((bf16[256,512]{1,0:T(8,128)(2,1)S(1)}, bf16[256,512]{1,0:T(8,128)(2,1)S(1)}, u32[]{:S(2)}, u32[]{:S(2)}) %collective-permute-start.40) | collective-permute-done | bytes 262176 | tf_op jit(solution)/shard_map/ppermute | solution.py:1066
  409.6 1.8 collective-permute-start.48
  411.4 3.7 collective-permute-start.47
  415.1 11.5 %collective-permute-done.53 = f32[264,128]{1,0:T(8,128)S(1)} collective-permute-done((f32[264,128]{1,0:T(8,128)S(1)}, f32[264,128]{1,0:T(8,128)S(1)}, u32[]{:S(2)}, u32[]{:S(2)}) %collective-permute-start.53) | collective-permute-done | bytes 135200 | tf_op jit(solution)/shard_map/ppermute | solution.py:1386
  428.7 4.3 collective-permute-start.43
  434.0 1.9 collective-permute-done.44
  437.4 2.1 collective-permute-start.49
  440.8 4.9 %collective-permute-done.49 = f32[128,128]{1,0:T(8,128)S(1)} collective-permute-done((f32[128,128]{1,0:T(8,128)S(1)}, f32[128,128]{1,0:T(8,128)S(1)}, u32[]{:S(2)}, u32[]{:S(2)}) %collective-permute-start.49) | collective-permute-done | bytes 65568 | tf_op jit(solution)/shard_map/ppermute | solution.py:1314
  446.9 2.3 copy.69
  (302 shorter events, 46.6 us)
Async XLA Ops:
  7.3 34.8 %all-to-all-start = ((bf16[8,64,1024]{2,1,0:T(8,128)(2,1)}), bf16[8,64,1024]{2,1,0:T(8,128)(2,1)S(1)}, u32[]{:S(2)}, u32[]{:S(2)}) async-start(bf16[8,64,1024]{2,1,0:T(8,128)(2,1)} %bitcast.145), calls=%async_computation | async-start | bytes 2097152 | tf_op jit(solution)/shard_map/all_to_all | solution.py:1108
  13.8 90.5 %copy-start.75 = (s32[8]{0:T(128)S(1)}, s32[8]{0:T(128)}, u32[]{:S(2)}) copy-start(s32[8]{0:T(128)} %param.35) | copy-start | bytes 100
  13.8 90.6 %copy-start.76 = (f32[8]{0:T(128)S(1)}, f32[8]{0:T(128)}, u32[]{:S(2)}) copy-start(f32[8]{0:T(128)} %param.30) | copy-start | bytes 100
  13.8 90.7 %copy-start.77 = (s32[24]{0:T(128)S(1)}, s32[24]{0:T(128)}, u32[]{:S(2)}) copy-start(s32[24]{0:T(128)} %param.33) | copy-start | bytes 292
  13.8 182.6 %all-gather.3.cloned.1.call-start = ((), (), s32[]{:S(2)}) async-start(), calls=%async_computation.5 | async-start | bytes 6801408 | tf_op jit(solution)/shard_map/all_gather | solution.py:1226
  13.9 28.0 %collective-permute-start.3 = (bf16[3,32,128]{2,1,0:T(8,128)(2,1)S(1)}, bf16[3,32,128]{2,1,0:T(8,128)(2,1)S(1)}, u32[]{:S(2)}, u32[]{:S(2)}) collective-permute-start(bf16[3,32,128]{2,1,0:T(8,128)(2,1)S(1)} %bitcast.170), channel_id=1, source_target_pairs={{0,0},{1,4},{2,8},{3,12},{4,16},{5,20},{6,24},{7,28},{8,1},{9,5},{... | collective-permute-start | bytes 73736 | tf_op jit(solution)/shard_map/ppermute | solution.py:1193
  18.1 23.9 %collective-permute-start.16 = (bf16[256,128]{1,0:T(8,128)(2,1)S(1)}, bf16[256,128]{1,0:T(8,128)(2,1)S(1)}, u32[]{:S(2)}, u32[]{:S(2)}) collective-permute-start(bf16[256,128]{1,0:T(8,128)(2,1)S(1)} %copy-done.57), channel_id=1, source_target_pairs={{0,2},{1,3},{2,0},{3,1},{4,6},{5,7},{6,4},{7,5},{8,10},{9,11},{10,... | collective-permute-start | bytes 196616 | tf_op jit(solution)/shard_map/ppermute | solution.py:1066
  20.6 11.4 %collective-permute-start.17 = (bf16[32,128]{1,0:T(8,128)(2,1)S(1)}, bf16[32,128]{1,0:T(8,128)(2,1)S(1)}, u32[]{:S(2)}, u32[]{:S(2)}) collective-permute-start(bf16[32,128]{1,0:T(8,128)(2,1)S(1)} %copy-done.74), channel_id=1, source_target_pairs={{0,0},{1,4},{2,8},{3,12},{4,16},{5,20},{6,24},{7,28},{8,1},{9,5},{... | collective-permute-start | bytes 24584 | tf_op jit(solution)/shard_map/ppermute | solution.py:1220
  22.5 21.2 %collective-permute-start.19 = (bf16[2,88,128]{2,1,0:T(8,128)(2,1)S(1)}, bf16[2,88,128]{2,1,0:T(8,128)(2,1)S(1)}, u32[]{:S(2)}, u32[]{:S(2)}) collective-permute-start(bf16[2,88,128]{2,1,0:T(8,128)(2,1)S(1)} %bitcast.169), channel_id=1, source_target_pairs={{0,0},{1,4},{2,8},{3,12},{4,16},{5,20},{6,24},{7,28},{8,1},{9,5},{... | collective-permute-start | bytes 135176 | tf_op jit(solution)/shard_map/ppermute | solution.py:1220
  25.0 18.7 %collective-permute-start.20 = (bf16[88,128]{1,0:T(8,128)(2,1)S(1)}, bf16[88,128]{1,0:T(8,128)(2,1)S(1)}, u32[]{:S(2)}, u32[]{:S(2)}) collective-permute-start(bf16[88,128]{1,0:T(8,128)(2,1)S(1)} %copy-done.73), channel_id=1, source_target_pairs={{0,0},{1,4},{2,8},{3,12},{4,16},{5,20},{6,24},{7,28},{8,1},{9,5},{... | collective-permute-start | bytes 67592 | tf_op jit(solution)/shard_map/ppermute | solution.py:1220
  32.0 11.7 %collective-permute-start.18 = (bf16[32,128]{1,0:T(8,128)(2,1)S(1)}, bf16[32,128]{1,0:T(8,128)(2,1)S(1)}, u32[]{:S(2)}, u32[]{:S(2)}) collective-permute-start(bf16[32,128]{1,0:T(8,128)(2,1)S(1)} %collective-permute-done.17), channel_id=1, source_target_pairs={{0,2},{1,3},{2,0},{3,1},{4,6},{5,7},{6,4},{7,5},{8,10},{9,11},{10,... | collective-permute-start | bytes 24584 | tf_op jit(solution)/shard_map/ppermute | solution.py:1066
  42.1 9.1 %collective-permute-start.9 = (bf16[1088,128]{1,0:T(8,128)(2,1)S(1)}, bf16[1088,128]{1,0:T(8,128)(2,1)S(1)}, u32[]{:S(2)}, u32[]{:S(2)}) collective-permute-start(bf16[1088,128]{1,0:T(8,128)(2,1)S(1)} %constant_dynamic-update-slice_fusion.refs_4_), channel_id=1, source_target_pairs={{0,24},{4,28},{8,16},{12,20},{16,8},{20,12},{24,0},{28,4},{1,25},{... | collective-permute-start | bytes 835592 | tf_op jit(solution)/shard_map/ppermute | solution.py:1071
  51.2 22.7 %collective-permute-start.5 = (bf16[1088,128]{1,0:T(8,128)(2,1)S(1)}, bf16[1088,128]{1,0:T(8,128)(2,1)S(1)}, u32[]{:S(2)}, u32[]{:S(2)}) collective-permute-start(bf16[1088,128]{1,0:T(8,128)(2,1)S(1)} %constant_dynamic-update-slice_fusion.refs_4_), channel_id=1, source_target_pairs={{0,8},{4,12},{8,0},{12,4},{16,24},{20,28},{24,16},{28,20},{1,9},{5... | collective-permute-start | bytes 835592 | tf_op jit(solution)/shard_map/ppermute | solution.py:1071
  56.8 20.0 %collective-permute-start.7 = (bf16[1088,128]{1,0:T(8,128)(2,1)S(1)}, bf16[1088,128]{1,0:T(8,128)(2,1)S(1)}, u32[]{:S(2)}, u32[]{:S(2)}) collective-permute-start(bf16[1088,128]{1,0:T(8,128)(2,1)S(1)} %constant_dynamic-update-slice_fusion.refs_4_), channel_id=1, source_target_pairs={{0,16},{4,20},{8,24},{12,28},{16,0},{20,4},{24,8},{28,12},{1,17},{... | collective-permute-start | bytes 835592 | tf_op jit(solution)/shard_map/ppermute | solution.py:1071
  57.7 19.1 %collective-permute-start.4 = (bf16[1088,128]{1,0:T(8,128)(2,1)S(1)}, bf16[1088,128]{1,0:T(8,128)(2,1)S(1)}, u32[]{:S(2)}, u32[]{:S(2)}) collective-permute-start(bf16[1088,128]{1,0:T(8,128)(2,1)S(1)} %constant_dynamic-update-slice_fusion.refs_4_), channel_id=1, source_target_pairs={{0,4},{4,0},{8,12},{12,8},{16,20},{20,16},{24,28},{28,24},{1,5},{5... | collective-permute-start | bytes 835592 | tf_op jit(solution)/shard_map/ppermute | solution.py:1071
  59.7 33.5 %collective-permute-start.1 = (bf16[512,1024]{1,0:T(8,128)(2,1)S(1)}, bf16[512,1024]{1,0:T(8,128)(2,1)}, u32[]{:S(2)}, u32[]{:S(2)}) collective-permute-start(bf16[512,1024]{1,0:T(8,128)(2,1)S(1)} %bitcast.125), channel_id=1, source_target_pairs={{0,2},{1,3},{2,0},{3,1},{4,6},{5,7},{6,4},{7,5},{8,10},{9,11},{10,... | collective-permute-start | bytes 3145736 | tf_op jit(solution)/shard_map/ppermute | solution.py:1066
  60.2 32.0 %collective-permute-start.10 = (bf16[1088,128]{1,0:T(8,128)(2,1)S(1)}, bf16[1088,128]{1,0:T(8,128)(2,1)S(1)}, u32[]{:S(2)}, u32[]{:S(2)}) collective-permute-start(bf16[1088,128]{1,0:T(8,128)(2,1)S(1)} %collective-permute-done.9.refs_10_), channel_id=1, source_target_pairs={{0,4},{4,0},{8,12},{12,8},{16,20},{20,16},{24,28},{28,24},{1,5},{5... | collective-permute-start | bytes 835592 | tf_op jit(solution)/shard_map/ppermute | solution.py:1071
  73.9 13.4 %collective-permute-start.6 = (bf16[1088,128]{1,0:T(8,128)(2,1)S(1)}, bf16[1088,128]{1,0:T(8,128)(2,1)S(1)}, u32[]{:S(2)}, u32[]{:S(2)}) collective-permute-start(bf16[1088,128]{1,0:T(8,128)(2,1)S(1)} %collective-permute-done.5.refs_6_), channel_id=1, source_target_pairs={{0,4},{4,0},{8,12},{12,8},{16,20},{20,16},{24,28},{28,24},{1,5},{5... | collective-permute-start | bytes 835592 | tf_op jit(solution)/shard_map/ppermute | solution.py:1071
  76.8 15.4 %collective-permute-start.8 = (bf16[1088,128]{1,0:T(8,128)(2,1)S(1)}, bf16[1088,128]{1,0:T(8,128)(2,1)S(1)}, u32[]{:S(2)}, u32[]{:S(2)}) collective-permute-start(bf16[1088,128]{1,0:T(8,128)(2,1)S(1)} %collective-permute-done.7.refs_8_), channel_id=1, source_target_pairs={{0,4},{4,0},{8,12},{12,8},{16,20},{20,16},{24,28},{28,24},{1,5},{5... | collective-permute-start | bytes 835592 | tf_op jit(solution)/shard_map/ppermute | solution.py:1071
  92.2 11.6 %collective-permute-start.12 = (bf16[8,224,128]{2,1,0:T(8,128)(2,1)S(1)}, bf16[8,224,128]{2,1,0:T(8,128)(2,1)S(1)}, u32[]{:S(2)}, u32[]{:S(2)}) collective-permute-start(bf16[8,224,128]{2,1,0:T(8,128)(2,1)S(1)} %constant_dynamic-update-slice_fusion.6.refs_12_.f0), channel_id=1, source_target_pairs={{0,2},{1,3},{2,0},{3,1},{4,6},{5,7},{6,4},{7,5},{8,10},{9,11},{10,... | collective-permute-start | bytes 1376264 | tf_op jit(solution)/shard_map/ppermute | solution.py:1066
  93.2 20.7 %collective-permute-start = (bf16[512,1024]{1,0:T(8,128)(2,1)S(1)}, bf16[512,1024]{1,0:T(8,128)(2,1)}, u32[]{:S(2)}, u32[]{:S(2)}) collective-permute-start(bf16[512,1024]{1,0:T(8,128)(2,1)S(1)} %bitcast.126), channel_id=1, source_target_pairs={{0,1},{1,0},{2,3},{3,2},{4,5},{5,4},{6,7},{7,6},{8,9},{9,8},{10,11... | collective-permute-start | bytes 3145736 | tf_op jit(solution)/shard_map/ppermute | solution.py:1066
  93.2 20.7 %collective-permute-start.2 = (bf16[512,1024]{1,0:T(8,128)(2,1)}, bf16[512,1024]{1,0:T(8,128)(2,1)}, u32[]{:S(2)}, u32[]{:S(2)}) collective-permute-start(bf16[512,1024]{1,0:T(8,128)(2,1)} %collective-permute-done.1.refs_2_), channel_id=1, source_target_pairs={{0,1},{1,0},{2,3},{3,2},{4,5},{5,4},{6,7},{7,6},{8,9},{9,8},{10,11... | collective-permute-start | bytes 3145736 | tf_op jit(solution)/shard_map/ppermute | solution.py:1066
  103.8 1.8 collective-permute-start.13
  103.8 10.1 %collective-permute-start.11 = (bf16[8,224,128]{2,1,0:T(8,128)(2,1)S(1)}, bf16[8,224,128]{2,1,0:T(8,128)(2,1)}, u32[]{:S(2)}, u32[]{:S(2)}) collective-permute-start(bf16[8,224,128]{2,1,0:T(8,128)(2,1)S(1)} %constant_dynamic-update-slice_fusion.6.refs_12_.f0), channel_id=1, source_target_pairs={{0,1},{1,0},{2,3},{3,2},{4,5},{5,4},{6,7},{7,6},{8,9},{9,8},{10,11... | collective-permute-start | bytes 1376264 | tf_op jit(solution)/shard_map/ppermute | solution.py:1066
  106.4 64.7 %all-to-all-start.1 = ((bf16[8,64,1024]{2,1,0:T(8,128)(2,1)}), bf16[8,64,1024]{2,1,0:T(8,128)(2,1)S(1)}, u32[]{:S(2)}, u32[]{:S(2)}) async-start(bf16[8,64,1024]{2,1,0:T(8,128)(2,1)} %bitcast.146), calls=%async_computation.1 | async-start | bytes 2097152 | tf_op jit(solution)/shard_map/all_to_all | solution.py:1108
  110.9 273.6 %reduce-scatter.4.cloned.1.call-start = ((), (), s32[]{:S(2)}) async-start(), calls=%async_computation.6 | async-start | bytes 2985984
  156.3 14.8 %collective-permute-start.14 = (bf16[1024,256]{1,0:T(8,128)(2,1)S(1)}, bf16[1024,256]{1,0:T(8,128)(2,1)S(1)}, u32[]{:S(2)}, u32[]{:S(2)}) collective-permute-start(bf16[1024,256]{1,0:T(8,128)(2,1)S(1)} %get-tuple-element.107), channel_id=1, source_target_pairs={{0,2},{1,3},{2,0},{3,1},{4,6},{5,7},{6,4},{7,5},{8,10},{9,11},{10,... | collective-permute-start | bytes 1572872 | tf_op jit(solution)/shard_map/ppermute | solution.py:1066
  171.1 25.3 %collective-permute-start.15 = (bf16[512,1024]{1,0:T(8,128)(2,1)S(1)}, bf16[512,1024]{1,0:T(8,128)(2,1)}, u32[]{:S(2)}, u32[]{:S(2)}) collective-permute-start(bf16[512,1024]{1,0:T(8,128)(2,1)S(1)} %bitcast.132), channel_id=1, source_target_pairs={{0,2},{1,3},{2,0},{3,1},{4,6},{5,7},{6,4},{7,5},{8,10},{9,11},{10,... | collective-permute-start | bytes 3145736 | tf_op jit(solution)/shard_map/ppermute | solution.py:1066
  208.0 2.7 collective-permute-start.21
  208.0 4.2 collective-permute-start.23
  211.4 74.7 %copy-start.9 = (bf16[512,1024]{1,0:T(8,128)(2,1)}, bf16[512,1024]{1,0:T(8,128)(2,1)S(1)}, u32[]{:S(2)}) copy-start(bf16[512,1024]{1,0:T(8,128)(2,1)S(1)} %get-tuple-element.118.refs_1_) | copy-start | bytes 3145732
  211.4 2.7 collective-permute-start.22
  211.7 25.4 %collective-permute-start.25 = (bf16[512,1024]{1,0:T(8,128)(2,1)S(1)}, bf16[512,1024]{1,0:T(8,128)(2,1)S(1)}, u32[]{:S(2)}, u32[]{:S(2)}) collective-permute-start(bf16[512,1024]{1,0:T(8,128)(2,1)S(1)} %get-tuple-element.121.x0.refs_0_), channel_id=1, source_target_pairs={{0,2},{1,3},{2,0},{3,1},{4,6},{5,7},{6,4},{7,5},{8,10},{9,11},{10,... | collective-permute-start | bytes 3145736 | tf_op jit(solution)/shard_map/ppermute | solution.py:1066
  211.9 25.1 %collective-permute-start.27 = (bf16[512,1024]{1,0:T(8,128)(2,1)}, bf16[512,1024]{1,0:T(8,128)(2,1)S(1)}, u32[]{:S(2)}, u32[]{:S(2)}) collective-permute-start(bf16[512,1024]{1,0:T(8,128)(2,1)} %collective-permute-done.15.g0.refs_6_), channel_id=1, source_target_pairs={{0,1},{1,0},{2,3},{3,2},{4,5},{5,4},{6,7},{7,6},{8,9},{9,8},{10,11... | collective-permute-start | bytes 3145736 | tf_op jit(solution)/shard_map/ppermute | solution.py:1066
  237.1 2.7 collective-permute-start.26
  257.8 2.7 collective-permute-start.28
  260.8 25.3 %collective-permute-start.29 = (bf16[512,1024]{1,0:T(8,128)(2,1)S(1)}, bf16[512,1024]{1,0:T(8,128)(2,1)S(1)}, u32[]{:S(2)}, u32[]{:S(2)}) collective-permute-start(bf16[512,1024]{1,0:T(8,128)(2,1)S(1)} %add_convert_fusion.3), channel_id=1, source_target_pairs={{0,2},{1,3},{2,0},{3,1},{4,6},{5,7},{6,4},{7,5},{8,10},{9,11},{10,... | collective-permute-start | bytes 3145736 | tf_op jit(solution)/shard_map/ppermute | solution.py:1066
  261.2 24.9 %collective-permute-start.24 = (bf16[512,1024]{1,0:T(8,128)(2,1)S(1)}, bf16[512,1024]{1,0:T(8,128)(2,1)S(1)}, u32[]{:S(2)}, u32[]{:S(2)}) collective-permute-start(bf16[512,1024]{1,0:T(8,128)(2,1)S(1)} %get-tuple-element.127), channel_id=1, source_target_pairs={{0,1},{1,0},{2,3},{3,2},{4,5},{5,4},{6,7},{7,6},{8,9},{9,8},{10,11... | collective-permute-start | bytes 3145736 | tf_op jit(solution)/shard_map/ppermute | solution.py:1066
  287.7 3.6 collective-permute-start.30
  287.8 12.1 %collective-permute-start.32 = (bf16[512,1024]{1,0:T(8,128)(2,1)}, bf16[512,1024]{1,0:T(8,128)(2,1)}, u32[]{:S(2)}, u32[]{:S(2)}) collective-permute-start(bf16[512,1024]{1,0:T(8,128)(2,1)} %get-tuple-element.156), channel_id=1, source_target_pairs={{0,1},{1,0},{2,3},{3,2},{4,5},{5,4},{6,7},{7,6},{8,9},{9,8},{10,11... | collective-permute-start | bytes 3145736 | tf_op jit(solution)/shard_map/ppermute | solution.py:1066
  296.1 14.0 %collective-permute-start.31 = (bf16[1024,256]{1,0:T(8,128)(2,1)S(1)}, bf16[1024,256]{1,0:T(8,128)(2,1)S(1)}, u32[]{:S(2)}, u32[]{:S(2)}) collective-permute-start(bf16[1024,256]{1,0:T(8,128)(2,1)S(1)} %get-tuple-element.154), channel_id=1, source_target_pairs={{0,2},{1,3},{2,0},{3,1},{4,6},{5,7},{6,4},{7,5},{8,10},{9,11},{10,... | collective-permute-start | bytes 1572872 | tf_op jit(solution)/shard_map/ppermute | solution.py:1066
  310.1 28.9 %collective-permute-start.33 = (bf16[512,1024]{1,0:T(8,128)(2,1)S(1)}, bf16[512,1024]{1,0:T(8,128)(2,1)S(1)}, u32[]{:S(2)}, u32[]{:S(2)}) collective-permute-start(bf16[512,1024]{1,0:T(8,128)(2,1)S(1)} %add_convert_fusion.2), channel_id=1, source_target_pairs={{0,2},{1,3},{2,0},{3,1},{4,6},{5,7},{6,4},{7,5},{8,10},{9,11},{10,... | collective-permute-start | bytes 3145736 | tf_op jit(solution)/shard_map/ppermute | solution.py:1066
  310.4 34.3 %collective-permute-start.36 = (bf16[512,1024]{1,0:T(8,128)(2,1)S(1)}, bf16[512,1024]{1,0:T(8,128)(2,1)S(1)}, u32[]{:S(2)}, u32[]{:S(2)}) collective-permute-start(bf16[512,1024]{1,0:T(8,128)(2,1)S(1)} %copy-done.48), channel_id=1, source_target_pairs={{0,1},{1,0},{2,3},{3,2},{4,5},{5,4},{6,7},{7,6},{8,9},{9,8},{10,11... | collective-permute-start | bytes 3145736 | tf_op jit(solution)/shard_map/ppermute | solution.py:1066
  342.9 4.1 collective-permute-start.34
  348.4 31.5 %all-to-all-start.2 = ((bf16[8,64,1024]{2,1,0:T(8,128)(2,1)}), bf16[8,64,1024]{2,1,0:T(8,128)(2,1)}, u32[]{:S(2)}, u32[]{:S(2)}) async-start(bf16[8,64,1024]{2,1,0:T(8,128)(2,1)} %bitcast.142), calls=%async_computation.2 | async-start | bytes 2097152 | tf_op jit(solution)/shard_map/all_to_all | solution.py:1108
  353.6 25.2 %collective-permute-start.35 = (bf16[512,1024]{1,0:T(8,128)(2,1)}, bf16[512,1024]{1,0:T(8,128)(2,1)}, u32[]{:S(2)}, u32[]{:S(2)}) collective-permute-start(bf16[512,1024]{1,0:T(8,128)(2,1)} %add_convert_fusion.1), channel_id=1, source_target_pairs={{0,2},{1,3},{2,0},{3,1},{4,6},{5,7},{6,4},{7,5},{8,10},{9,11},{10,... | collective-permute-start | bytes 3145736 | tf_op jit(solution)/shard_map/ppermute | solution.py:1066
  362.3 17.6 %collective-permute-start.37 = (bf16[512,1024]{1,0:T(8,128)(2,1)}, bf16[512,1024]{1,0:T(8,128)(2,1)}, u32[]{:S(2)}, u32[]{:S(2)}) collective-permute-start(bf16[512,1024]{1,0:T(8,128)(2,1)} %get-tuple-element.181), channel_id=1, source_target_pairs={{0,1},{1,0},{2,3},{3,2},{4,5},{5,4},{6,7},{7,6},{8,9},{9,8},{10,11... | collective-permute-start | bytes 3145736 | tf_op jit(solution)/shard_map/ppermute | solution.py:1066
  386.4 60.4 %all-to-all-start.3 = ((bf16[8,64,1024]{2,1,0:T(8,128)(2,1)}), bf16[8,64,1024]{2,1,0:T(8,128)(2,1)S(1)}, u32[]{:S(2)}, u32[]{:S(2)}) async-start(bf16[8,64,1024]{2,1,0:T(8,128)(2,1)} %bitcast.34), calls=%async_computation.3 | async-start | bytes 2097152 | tf_op jit(solution)/shard_map/all_to_all | solution.py:1108
  391.5 4.8 %collective-permute-start.39 = (bf16[256,512]{1,0:T(8,128)(2,1)S(1)}, bf16[256,512]{1,0:T(8,128)(2,1)S(1)}, u32[]{:S(2)}, u32[]{:S(2)}) collective-permute-start(bf16[256,512]{1,0:T(8,128)(2,1)S(1)} %get-tuple-element.199), channel_id=1, source_target_pairs={{0,1},{1,0},{2,3},{3,2},{4,5},{5,4},{6,7},{7,6},{8,9},{9,8},{10,11... | collective-permute-start | bytes 786440 | tf_op jit(solution)/shard_map/ppermute | solution.py:1066
  391.6 12.9 %collective-permute-start.38 = (bf16[256,512]{1,0:T(8,128)(2,1)S(1)}, bf16[256,512]{1,0:T(8,128)(2,1)S(1)}, u32[]{:S(2)}, u32[]{:S(2)}) collective-permute-start(bf16[256,512]{1,0:T(8,128)(2,1)S(1)} %get-tuple-element.198), channel_id=1, source_target_pairs={{0,1},{1,0},{2,3},{3,2},{4,5},{5,4},{6,7},{7,6},{8,9},{9,8},{10,11... | collective-permute-start | bytes 786440 | tf_op jit(solution)/shard_map/ppermute | solution.py:1066
  392.2 1.4 collective-permute-start.51
  392.4 17.2 %collective-permute-start.41 = (bf16[8,32,128]{2,1,0:T(8,128)(2,1)S(1)}, bf16[8,32,128]{2,1,0:T(8,128)(2,1)S(1)}, u32[]{:S(2)}, u32[]{:S(2)}) collective-permute-start(bf16[8,32,128]{2,1,0:T(8,128)(2,1)S(1)} %bitcast.161), channel_id=1, source_target_pairs={{0,2},{1,3},{2,0},{3,1},{4,6},{5,7},{6,4},{7,5},{8,10},{9,11},{10,... | collective-permute-start | bytes 196616 | tf_op jit(solution)/shard_map/ppermute | solution.py:1066
  393.4 6.8 %collective-permute-start.50 = (f32[96,128]{1,0:T(8,128)S(1)}, f32[96,128]{1,0:T(8,128)S(1)}, u32[]{:S(2)}, u32[]{:S(2)}) collective-permute-start(f32[96,128]{1,0:T(8,128)S(1)} %get-tuple-element.207), channel_id=1, source_target_pairs={{0,1},{1,0},{2,3},{3,2},{4,5},{5,4},{6,7},{7,6},{8,9},{9,8},{10,11... | collective-permute-start | bytes 147464 | tf_op jit(solution)/shard_map/ppermute | solution.py:1066
  393.6 32.9 %collective-permute-start.53 = (f32[264,128]{1,0:T(8,128)S(1)}, f32[264,128]{1,0:T(8,128)S(1)}, u32[]{:S(2)}, u32[]{:S(2)}) collective-permute-start(f32[264,128]{1,0:T(8,128)S(1)} %slice.165), channel_id=1, source_target_pairs={{0,0},{4,1},{8,2},{12,3},{16,4},{20,5},{24,6},{28,7},{1,8},{5,9},{... | collective-permute-start | bytes 405512 | tf_op jit(solution)/shard_map/ppermute | solution.py:1386
  396.4 6.1 %collective-permute-start.52 = (f32[96,128]{1,0:T(8,128)S(1)}, f32[96,128]{1,0:T(8,128)S(1)}, u32[]{:S(2)}, u32[]{:S(2)}) collective-permute-start(f32[96,128]{1,0:T(8,128)S(1)} %slice_add_fusion), channel_id=1, source_target_pairs={{0,2},{1,3},{2,0},{3,1},{4,6},{5,7},{6,4},{7,5},{8,10},{9,11},{10,... | collective-permute-start | bytes 147464 | tf_op jit(solution)/shard_map/ppermute | solution.py:1066
  400.2 9.0 %collective-permute-start.40 = (bf16[256,512]{1,0:T(8,128)(2,1)S(1)}, bf16[256,512]{1,0:T(8,128)(2,1)S(1)}, u32[]{:S(2)}, u32[]{:S(2)}) collective-permute-start(bf16[256,512]{1,0:T(8,128)(2,1)S(1)} %fusion), channel_id=1, source_target_pairs={{0,2},{1,3},{2,0},{3,1},{4,6},{5,7},{6,4},{7,5},{8,10},{9,11},{10,... | collective-permute-start | bytes 786440 | tf_op jit(solution)/shard_map/ppermute | solution.py:1066
  409.6 19.1 %collective-permute-start.48 = (bf16[256,128]{1,0:T(8,128)(2,1)S(1)}, bf16[256,128]{1,0:T(8,128)(2,1)S(1)}, u32[]{:S(2)}, u32[]{:S(2)}) collective-permute-start(bf16[256,128]{1,0:T(8,128)(2,1)S(1)} %get-tuple-element.201), channel_id=1, source_target_pairs={{0,28},{4,24},{8,20},{12,16},{16,12},{20,8},{24,4},{28,0},{1,29},{... | collective-permute-start | bytes 196616 | tf_op jit(solution)/shard_map/ppermute | solution.py:1071
  411.4 21.6 %collective-permute-start.47 = (bf16[256,128]{1,0:T(8,128)(2,1)S(1)}, bf16[256,128]{1,0:T(8,128)(2,1)S(1)}, u32[]{:S(2)}, u32[]{:S(2)}) collective-permute-start(bf16[256,128]{1,0:T(8,128)(2,1)S(1)} %get-tuple-element.202), channel_id=1, source_target_pairs={{0,24},{4,28},{8,16},{12,20},{16,8},{20,12},{24,0},{28,4},{1,25},{... | collective-permute-start | bytes 196616 | tf_op jit(solution)/shard_map/ppermute | solution.py:1071
  427.2 6.9 %collective-permute-start.46 = (bf16[256,128]{1,0:T(8,128)(2,1)S(1)}, bf16[256,128]{1,0:T(8,128)(2,1)S(1)}, u32[]{:S(2)}, u32[]{:S(2)}) collective-permute-start(bf16[256,128]{1,0:T(8,128)(2,1)S(1)} %get-tuple-element.203), channel_id=1, source_target_pairs={{0,20},{4,16},{8,28},{12,24},{16,4},{20,0},{24,12},{28,8},{1,21},{... | collective-permute-start | bytes 196616 | tf_op jit(solution)/shard_map/ppermute | solution.py:1071
  427.2 6.9 %collective-permute-start.45 = (bf16[256,128]{1,0:T(8,128)(2,1)S(1)}, bf16[256,128]{1,0:T(8,128)(2,1)S(1)}, u32[]{:S(2)}, u32[]{:S(2)}) collective-permute-start(bf16[256,128]{1,0:T(8,128)(2,1)S(1)} %get-tuple-element.204), channel_id=1, source_target_pairs={{0,16},{4,20},{8,24},{12,28},{16,0},{20,4},{24,8},{28,12},{1,17},{... | collective-permute-start | bytes 196616 | tf_op jit(solution)/shard_map/ppermute | solution.py:1071
  427.7 8.2 %collective-permute-start.44 = (bf16[256,128]{1,0:T(8,128)(2,1)S(1)}, bf16[256,128]{1,0:T(8,128)(2,1)S(1)}, u32[]{:S(2)}, u32[]{:S(2)}) collective-permute-start(bf16[256,128]{1,0:T(8,128)(2,1)S(1)} %get-tuple-element.205), channel_id=1, source_target_pairs={{0,12},{4,8},{8,4},{12,0},{16,28},{20,24},{24,20},{28,16},{1,13},{... | collective-permute-start | bytes 196616 | tf_op jit(solution)/shard_map/ppermute | solution.py:1071
  428.7 7.9 %collective-permute-start.43 = (bf16[256,128]{1,0:T(8,128)(2,1)S(1)}, bf16[256,128]{1,0:T(8,128)(2,1)S(1)}, u32[]{:S(2)}, u32[]{:S(2)}) collective-permute-start(bf16[256,128]{1,0:T(8,128)(2,1)S(1)} %get-tuple-element.206), channel_id=1, source_target_pairs={{0,8},{4,12},{8,0},{12,4},{16,24},{20,28},{24,16},{28,20},{1,9},{5... | collective-permute-start | bytes 196616 | tf_op jit(solution)/shard_map/ppermute | solution.py:1071
  433.0 4.3 collective-permute-start.42
  437.4 8.2 %collective-permute-start.49 = (f32[128,128]{1,0:T(8,128)S(1)}, f32[128,128]{1,0:T(8,128)S(1)}, u32[]{:S(2)}, u32[]{:S(2)}) collective-permute-start(f32[128,128]{1,0:T(8,128)S(1)} %slice.186), channel_id=1, source_target_pairs={{0,0},{4,1},{8,2},{12,3},{16,4},{20,5},{24,6},{28,7},{1,8},{5,9},{... | collective-permute-start | bytes 196616 | tf_op jit(solution)/shard_map/ppermute | solution.py:1314
  (75 other events, 1274.0 us)
Sparse Core Ops, SparseCore 0:
  51.3 125.1 all-gather.2
  288.4 70.6 reduce-scatter.3
where the time goes:
time: 466 us; the launch traced here: 457 us
  waiting for transfers between devices  160 us (34%)
  Pallas kernels  151 us (32%)
  starting transfers between devices  89.7 us (19%)
  local copies, waits for them, and re-layouts  31.3 us (7%)
  between operations  17 us (4%)
  other arithmetic  8.34 us (2%)
    ppermute x34, waiting for transfers between devices, swap(): return lax.ppermute(values, 'tensor', [(i, i ^ bit) for i in range(size)])  100 us
    ppermute x14, waiting for transfers between devices, swap_dp(): return lax.ppermute(values, 'dp', [(i, i ^ bits) for i in range(size)])  39.6 us
    pallas_call x2, Pallas kernels, ffn(): pl.pallas_call(functools.partial(ffn_kernel, first), grid_spec=pltpu.Pref...  32 us
    pallas_call x1, Pallas kernels, mixer_backward(): pl.pallas_call(functools.partial(mixer_backward_kernel, spans, blocks), g...  28.5 us
    ppermute x34, starting transfers between devices, swap(): return lax.ppermute(values, 'tensor', [(i, i ^ bit) for i in range(size)])  27.7 us
    ppermute x14, starting transfers between devices, swap_dp(): return lax.ppermute(values, 'dp', [(i, i ^ bits) for i in range(size)])  24.7 us
    unnamed x187, local copies, waits for them, and re-layouts  22.3 us
    all_to_all x4, starting transfers between devices, exchange_dp(): return lax.all_to_all(values, 'dp', split_axis=0, concat_axis=0, tiled=True)  21 us
  transfers between devices with their start and end apart: 60, of which 29 were waited for; matrix products, arithmetic and copies ran while one was open for 3% of the time, Pallas kernels for 28%

commit v1 on v0

--- a/solution.py
+++ b/solution.py
@@ -1194,7 +1194,7 @@
             query_key_value_lower,
             *fulls,
         )
-        slabs = gather_slabs(after(pack, arrived))
+        slabs = gather_slabs(pack)
         lower_rows = pack.shape[0] - 7 * share
         mates = gather_tensor(jnp.stack([v[lower_rows:] for v in slabs]))
     else:

time: 466 us -> 509 us (1.092)
  waiting for transfers between devices: 160 us -> 205 us
  starting transfers between devices: 89.7 us -> 80 us
    ppermute x14, waiting for transfers between devices: 39.6 us -> 80.4 us  [swap_dp(): return lax.ppermute(values, 'dp', [(i, i ^ bits) for i in range(size)])]
    ppermute x34, waiting for transfers between devices: 100 us -> 107 us  [swap(): return lax.ppermute(values, 'tensor', [(i, i ^ bit) for i in range(size)])]
    ppermute x14, starting transfers between devices: 24.7 us -> 17.9 us  [swap_dp(): return lax.ppermute(values, 'dp', [(i, i ^ bits) for i in range(size)])]
    unnamed x187 -> x170, local copies, waits for them, and re-layouts: 22.3 us -> 27.3 us
  transfers between devices with their start and end apart: 60 -> 60, of which waited for: 29 -> 29; matrix products, arithmetic and copies ran while one was open for 3% -> 4% of each run, Pallas kernels for 28% -> 26%
where the time goes in v1:
time: 509 us; the launch traced here: 499 us
  waiting for transfers between devices  205 us (40%)
  Pallas kernels  153 us (30%)
  starting transfers between devices  80 us (16%)
  local copies, waits for them, and re-layouts  36.3 us (7%)
  between operations  16.9 us (3%)
  other arithmetic  8.35 us (2%)
    ppermute x34, waiting for transfers between devices, swap(): return lax.ppermute(values, 'tensor', [(i, i ^ bit) for i in range(size)])  107 us
    ppermute x14, waiting for transfers between devices, swap_dp(): return lax.ppermute(values, 'dp', [(i, i ^ bits) for i in range(size)])  80.4 us
    pallas_call x2, Pallas kernels, ffn(): pl.pallas_call(functools.partial(ffn_kernel, first), grid_spec=pltpu.Pref...  32 us
    pallas_call x1, Pallas kernels, mixer_backward(): pl.pallas_call(functools.partial(mixer_backward_kernel, spans, blocks), g...  29.8 us
    unnamed x170, local copies, waits for them, and re-layouts  27.3 us
    ppermute x34, starting transfers between devices, swap(): return lax.ppermute(values, 'tensor', [(i, i ^ bit) for i in range(size)])  23.5 us
    all_to_all x4, starting transfers between devices, exchange_dp(): return lax.all_to_all(values, 'dp', split_axis=0, concat_axis=0, tiled=True)  22.6 us
    ppermute x14, starting transfers between devices, swap_dp(): return lax.ppermute(values, 'dp', [(i, i ^ bits) for i in range(size)])  17.9 us
  transfers between devices with their start and end apart: 60, of which 29 were waited for; matrix products, arithmetic and copies ran while one was open for 4% of the time, Pallas kernels for 26%

profile of v1, /device:TPU:2, one launch (start us, length us, event | category | flops | bytes accessed | tf_op | source)
XLA Modules:
  0.0 499.3 jit_solution(13351389103973229210)
XLA Ops:
  7.3 4.6 collective-permute-start.3
  11.9 2.5 collective-permute-start.16
  14.4 1.9 collective-permute-start.17
  16.3 2.3 collective-permute-start.19
  18.6 3.4 collective-permute-start.20
  24.9 5.0 %collective-permute-start.18 = (bf16[32,128]{1,0:T(8,128)(2,1)S(1)}, bf16[32,128]{1,0:T(8,128)(2,1)S(1)}, u32[]{:S(2)}, u32[]{:S(2)}) collective-permute-start(bf16[32,128]{1,0:T(8,128)(2,1)S(1)} %collective-permute-done.17), channel_id=1, source_target_pairs={{0,2},{1,3},{2,0},{3,1},{4,6},{5,7},{6,4},{7,5},{8,10},{9,11},{10,... | collective-permute-start | bytes 24584 | tf_op jit(solution)/shard_map/ppermute | solution.py:1066
  31.6 7.6 %collective-permute-done.9.refs_10_ = bf16[1088,128]{1,0:T(8,128)(2,1)S(1)} collective-permute-done((bf16[1088,128]{1,0:T(8,128)(2,1)S(1)}, bf16[1088,128]{1,0:T(8,128)(2,1)S(1)}, u32[]{:S(2)}, u32[]{:S(2)}) %collective-permute-start.9) | collective-permute-done | bytes 278560 | tf_op jit(solution)/shard_map/ppermute | solution.py:1071
  39.3 6.6 %all-to-all-start = ((bf16[8,64,1024]{2,1,0:T(8,128)(2,1)}), bf16[8,64,1024]{2,1,0:T(8,128)(2,1)S(1)}, u32[]{:S(2)}, u32[]{:S(2)}) async-start(bf16[8,64,1024]{2,1,0:T(8,128)(2,1)} %bitcast.2), calls=%async_computation | async-start | bytes 2097152 | tf_op jit(solution)/shard_map/all_to_all | solution.py:1108
  46.0 1.5 collective-permute-start.5
  47.5 2.4 collective-permute-start.7
  50.4 1.5 collective-permute-start.10
  51.9 38.6 %collective-permute-done.5.refs_6_ = bf16[1088,128]{1,0:T(8,128)(2,1)S(1)} collective-permute-done((bf16[1088,128]{1,0:T(8,128)(2,1)S(1)}, bf16[1088,128]{1,0:T(8,128)(2,1)S(1)}, u32[]{:S(2)}, u32[]{:S(2)}) %collective-permute-start.5) | collective-permute-done | bytes 278560 | tf_op jit(solution)/shard_map/ppermute | solution.py:1071
  90.5 18.1 %collective-permute-done.7.refs_8_ = bf16[1088,128]{1,0:T(8,128)(2,1)S(1)} collective-permute-done((bf16[1088,128]{1,0:T(8,128)(2,1)S(1)}, bf16[1088,128]{1,0:T(8,128)(2,1)S(1)}, u32[]{:S(2)}, u32[]{:S(2)}) %collective-permute-start.7) | collective-permute-done | bytes 278560 | tf_op jit(solution)/shard_map/ppermute | solution.py:1071
  111.1 12.5 %collective-permute-done.8.refs_9_ = bf16[1088,128]{1,0:T(8,128)(2,1)} collective-permute-done((bf16[1088,128]{1,0:T(8,128)(2,1)S(1)}, bf16[1088,128]{1,0:T(8,128)(2,1)}, u32[]{:S(2)}, u32[]{:S(2)}) %collective-permute-start.8) | collective-permute-done | bytes 278560 | tf_op jit(solution)/shard_map/ppermute | solution.py:1071
  124.9 11.5 %collective-permute-done.1.refs_2_ = bf16[512,1024]{1,0:T(8,128)(2,1)} collective-permute-done((bf16[512,1024]{1,0:T(8,128)(2,1)S(1)}, bf16[512,1024]{1,0:T(8,128)(2,1)}, u32[]{:S(2)}, u32[]{:S(2)}) %collective-permute-start.1) | collective-permute-done | bytes 1048608 | tf_op jit(solution)/shard_map/ppermute | solution.py:1066
  136.4 8.3 %collective-permute-done.12.refs_14_.f2 = bf16[8,224,128]{2,1,0:T(8,128)(2,1)S(1)} collective-permute-done((bf16[8,224,128]{2,1,0:T(8,128)(2,1)S(1)}, bf16[8,224,128]{2,1,0:T(8,128)(2,1)S(1)}, u32[]{:S(2)}, u32[]{:S(2)}) %collective-permute-start.12) | collective-permute-done | bytes 458784 | tf_op jit(solution)/shard_map/ppermute | solution.py:1066
  145.5 1.7 collective-permute-done.13.refs_15_.f3
  148.0 4.8 all-to-all-start.1
  155.8 14.4 %project_qkv.1 = (bf16[2048,1024]{1,0:T(8,128)(2,1)}, bf16[3,2048,256]{2,1,0:T(8,128)(2,1)}, bf16[2048,384]{1,0:T(8,128)(2,1)}, bf16[3,1024,256]{2,1,0:T(8,128)(...) custom-call(s32[9]{0:T(128)S(1)} %concatenate.21.meta, bf16[512,1024]{1,0:T(8,128)(2,1)} %bitcast.129, ...), custom_call_target="tpu_custom_call" | custom-call | flops 5737807872 | bytes 8388608 | tf_op jit(solution)/shard_map/project_qkv/pallas_call | solution.py:139
  170.2 16.4 %attend_forward.1 = (bf16[2048,256]{1,0:T(8,128)(2,1)S(1)}, f32[8,8,256]{2,1,0:T(8,128)S(1)}) custom-call(s32[9]{0:T(128)S(1)} %concatenate.21.meta, bf16[3,2048,256]{2,1,0:T(8,128)(2,1)} %get-tuple-element.102.rows_in.qkv), custom_call_target="tpu_custom_call" | custom-call | flops 4000000000 | bytes 12000000 | tf_op jit(solution)/shard_map/attend_forward/pallas_call | solution.py:255
  187.6 11.7 %memory_forward.1 = (bf16[1024,256]{1,0:T(8,128)(2,1)S(1)}, bf16[1024,256]{1,0:T(8,128)(2,1)}, bf16[32,2,128,128]{3,2,1,0:T(8,128)(2,1)}) custom-call(s32[9]{0:T(128)S(1)} %concatenate.21.meta, f32[4]{0:T(128)S(1)} %pad_maximum_fusion.1.fmeta, bf16[3,2048,256]{2,1,0:T(8,128)(2,1)} %get-tuple-element.102.rows_in.qkv, bf16[2048,256]{1,0:T(8,128)(2,1)} %copy-done.16), custom_call_target="tpu_custom_call" | custom-call | flops 100000 | bytes 100000 | tf_op jit(solution)/shard_map/memory_forward/pallas_call | solution.py:335
  200.3 13.1 %collective-permute-done.14.far = bf16[1024,256]{1,0:T(8,128)(2,1)S(1)} collective-permute-done((bf16[1024,256]{1,0:T(8,128)(2,1)}, bf16[1024,256]{1,0:T(8,128)(2,1)S(1)}, u32[]{:S(2)}, u32[]{:S(2)}) %collective-permute-start.14) | collective-permute-done | bytes 524320 | tf_op jit(solution)/shard_map/ppermute | solution.py:1066
  214.1 23.4 %collective-permute-done.15.g0.refs_6_ = bf16[512,1024]{1,0:T(8,128)(2,1)} collective-permute-done((bf16[512,1024]{1,0:T(8,128)(2,1)S(1)}, bf16[512,1024]{1,0:T(8,128)(2,1)}, u32[]{:S(2)}, u32[]{:S(2)}) %collective-permute-start.15) | collective-permute-done | bytes 1048608 | tf_op jit(solution)/shard_map/ppermute | solution.py:1066
  238.7 2.7 copy-done.5
  242.4 2.8 unpack.1
  245.3 2.9 out_forward.1
  249.7 2.1 collective-permute-done.21.got
  253.6 1.7 collective-permute-done.22.x1.refs_1_
  255.3 15.2 %ffn.2 = (bf16[512,1024]{1,0:T(8,128)(2,1)S(1)}, bf16[512,1024]{1,0:T(8,128)(2,1)S(1)}, bf16[1024,704]{1,0:T(8,128)(2,1)}, bf16[2,1024,704]{2,1,0:T(8,128)(2,1)}...) custom-call(s32[9]{0:T(128)S(1)} %concatenate.21.meta, ...), custom_call_target="tpu_custom_call" | custom-call | flops 8858370048 | bytes 14000000 | tf_op jit(solution)/shard_map/ffn/pallas_call | solution.py:785
  270.5 7.7 %collective-permute-done.25.x0.refs_2_ = bf16[512,1024]{1,0:T(8,128)(2,1)S(1)} collective-permute-done((bf16[512,1024]{1,0:T(8,128)(2,1)S(1)}, bf16[512,1024]{1,0:T(8,128)(2,1)S(1)}, u32[]{:S(2)}, u32[]{:S(2)}) %collective-permute-start.25) | collective-permute-done | bytes 1048608 | tf_op jit(solution)/shard_map/ppermute | solution.py:1066
  278.3 2.7 collective-permute-done.26.x1.refs_3_
  280.9 16.8 %ffn.3 = (bf16[512,1024]{1,0:T(8,128)(2,1)S(1)}, bf16[512,1024]{1,0:T(8,128)(2,1)S(1)}, bf16[1024,704]{1,0:T(8,128)(2,1)}, bf16[2,1024,704]{2,1,0:T(8,128)(2,1)}...) custom-call(s32[9]{0:T(128)S(1)} %concatenate.21.meta, ...), custom_call_target="tpu_custom_call" | custom-call | flops 8858370048 | bytes 14000000 | tf_op jit(solution)/shard_map/ffn/pallas_call | solution.py:785
  299.0 2.5 collective-permute-done.28
  302.8 15.9 %ffn_rest.1 = (bf16[512,1024]{1,0:T(8,128)(2,1)S(1)}, bf16[512,1024]{1,0:T(8,128)(2,1)S(1)}, bf16[512,1024]{1,0:T(8,128)(2,1)S(1)}, bf16[512,1024]{1,0:T(8,128)(2,1)}, f32[8,648,128]{2,1,0:T(8,128)}) custom-call(s32[9]{0:T(128)S(1)} %concatenate.21.meta, bf16[512,1024]{1,0:T(8,128)(2,1)S(1)} %get-tuple-element.119.x0.refs_0_, ...), custom_call_target="tpu_custom_call" | custom-call | flops 6791416832 | bytes 30000000 | tf_op jit(solution)/shard_map/ffn_rest/pallas_call | solution.py:879
  318.7 8.5 %collective-permute-done.29.refs_4_ = bf16[512,1024]{1,0:T(8,128)(2,1)S(1)} collective-permute-done((bf16[512,1024]{1,0:T(8,128)(2,1)S(1)}, bf16[512,1024]{1,0:T(8,128)(2,1)S(1)}, u32[]{:S(2)}, u32[]{:S(2)}) %collective-permute-start.29) | collective-permute-done | bytes 1048608 | tf_op jit(solution)/shard_map/ppermute | solution.py:1066
  327.2 1.6 norm_gradient.2.grad_own.refs_0_
  329.5 2.9 collective-permute-done.30.grad_mate
  333.4 3.8 out_backward.1
  338.1 2.7 out_pairs.1
  341.5 1.8 add_convert_fusion.2
  343.3 7.9 %collective-permute-done.31.grad_far = bf16[1024,256]{1,0:T(8,128)(2,1)S(1)} collective-permute-done((bf16[1024,256]{1,0:T(8,128)(2,1)S(1)}, bf16[1024,256]{1,0:T(8,128)(2,1)S(1)}, u32[]{:S(2)}, u32[]{:S(2)}) %collective-permute-start.31) | collective-permute-done | bytes 524320 | tf_op jit(solution)/shard_map/ppermute | solution.py:1066
  352.1 29.8 %mixer_backward.1.grads0.grads1.grads = bf16[3,2048,256]{2,1,0:T(8,128)(2,1)S(1)} custom-call(s32[9]{0:T(128)S(1)} %concatenate.21.meta, f32[4]{0:T(128)S(1)} %pad_maximum_fusion.1.fmeta, bf16[3,2048,256]{2,1,0:T(8,128)(2,1)S(1)} %copy-done.13, bf16[1024,256]{1,0:T(8,128)(2,1)S(1)} %get-tuple-element.151.grad_near, ...), custom_call_target="tpu_custom_call" | custom-call | flops 10000000000 | bytes 16000000 | tf_op jit(solution)/shard_map/mixer_backward/pallas_call | solution.py:513
  381.9 3.8 qkv_backward.2
  386.3 1.9 add_convert_fusion
  388.6 1.4 add_convert_fusion.1
  390.0 6.0 %all-to-all-start.2 = ((bf16[8,64,1024]{2,1,0:T(8,128)(2,1)}), bf16[8,64,1024]{2,1,0:T(8,128)(2,1)}, u32[]{:S(2)}, u32[]{:S(2)}) async-start(bf16[8,64,1024]{2,1,0:T(8,128)(2,1)} %bitcast.144), calls=%async_computation.2 | async-start | bytes 2097152 | tf_op jit(solution)/shard_map/all_to_all | solution.py:1108
  399.9 4.8 qkv_backward.3
  405.7 2.2 copy-done.8
  409.3 5.1 %qkv_pairs.1 = (bf16[4,256,384]{2,1,0:T(8,128)(2,1)S(1)}, bf16[3,256,128]{2,1,0:T(8,128)(2,1)S(1)}) custom-call(s32[9]{0:T(128)S(1)} %concatenate.21.meta, bf16[2048,1024]{1,0:T(8,128)(2,1)S(1)} %copy-done.8, bf16[2048,384]{1,0:T(8,128)(2,1)S(1)} %copy-done.15, bf16[3,2048,256]{2,1,0:T(8,128)(2,1)S(1)} %mixer_backward.1.grads0.grads1.grads, ...), custom_call_target="tpu_custom_call" | custom-call | flops 83886080 | bytes 400000 | tf_op jit(solution)/shard_map/qkv_pairs/pallas_call | solution.py:975
  416.1 5.1 %collective-permute-done.35.refs_4_ = bf16[512,1024]{1,0:T(8,128)(2,1)} collective-permute-done((bf16[512,1024]{1,0:T(8,128)(2,1)}, bf16[512,1024]{1,0:T(8,128)(2,1)}, u32[]{:S(2)}, u32[]{:S(2)}) %collective-permute-start.35) | collective-permute-done | bytes 1048608 | tf_op jit(solution)/shard_map/ppermute | solution.py:1066
  422.1 4.7 norm_gradient.3
  428.7 5.1 %all-to-all-start.3 = ((bf16[8,64,1024]{2,1,0:T(8,128)(2,1)}), bf16[8,64,1024]{2,1,0:T(8,128)(2,1)S(1)}, u32[]{:S(2)}, u32[]{:S(2)}) async-start(bf16[8,64,1024]{2,1,0:T(8,128)(2,1)} %bitcast.34), calls=%async_computation.3 | async-start | bytes 2097152 | tf_op jit(solution)/shard_map/all_to_all | solution.py:1108
  436.4 1.9 collective-permute-start.53
  439.1 3.8 collective-permute-start.52
  443.1 2.1 collective-permute-done.52
  447.2 4.8 collective-permute-done.40
  452.4 2.0 collective-permute-start.48
  454.4 3.4 collective-permute-start.47
  457.7 11.0 %collective-permute-done.53 = f32[264,128]{1,0:T(8,128)S(1)} collective-permute-done((f32[264,128]{1,0:T(8,128)S(1)}, f32[264,128]{1,0:T(8,128)S(1)}, u32[]{:S(2)}, u32[]{:S(2)}) %collective-permute-start.53) | collective-permute-done | bytes 135200 | tf_op jit(solution)/shard_map/ppermute | solution.py:1386
  470.7 4.6 collective-permute-start.43
  476.2 1.7 collective-permute-done.44
  479.6 1.9 collective-permute-start.49
  482.7 4.8 collective-permute-done.49
  488.8 2.3 copy.69
  (286 shorter events, 51.9 us)
Async XLA Ops:
  7.2 230.3 %all-gather.3.cloned.1.call-start = ((), (), s32[]{:S(2)}) async-start(), calls=%async_computation.5 | async-start | bytes 6801408 | tf_op jit(solution)/shard_map/all_gather | solution.py:1226
  7.3 22.7 %collective-permute-start.3 = (bf16[3,32,128]{2,1,0:T(8,128)(2,1)}, bf16[3,32,128]{2,1,0:T(8,128)(2,1)S(1)}, u32[]{:S(2)}, u32[]{:S(2)}) collective-permute-start(bf16[3,32,128]{2,1,0:T(8,128)(2,1)} %bitcast.175), channel_id=1, source_target_pairs={{0,0},{1,4},{2,8},{3,12},{4,16},{5,20},{6,24},{7,28},{8,1},{9,5},{... | collective-permute-start | bytes 73736 | tf_op jit(solution)/shard_map/ppermute | solution.py:1193
  11.9 19.0 %collective-permute-start.16 = (bf16[256,128]{1,0:T(8,128)(2,1)}, bf16[256,128]{1,0:T(8,128)(2,1)S(1)}, u32[]{:S(2)}, u32[]{:S(2)}) collective-permute-start(bf16[256,128]{1,0:T(8,128)(2,1)} %param.27), channel_id=1, source_target_pairs={{0,2},{1,3},{2,0},{3,1},{4,6},{5,7},{6,4},{7,5},{8,10},{9,11},{10,... | collective-permute-start | bytes 196616 | tf_op jit(solution)/shard_map/ppermute | solution.py:1066
  14.4 10.5 %collective-permute-start.17 = (bf16[32,128]{1,0:T(8,128)(2,1)}, bf16[32,128]{1,0:T(8,128)(2,1)S(1)}, u32[]{:S(2)}, u32[]{:S(2)}) collective-permute-start(bf16[32,128]{1,0:T(8,128)(2,1)} %param.38), channel_id=1, source_target_pairs={{0,0},{1,4},{2,8},{3,12},{4,16},{5,20},{6,24},{7,28},{8,1},{9,5},{... | collective-permute-start | bytes 24584 | tf_op jit(solution)/shard_map/ppermute | solution.py:1220
  16.3 15.3 %collective-permute-start.19 = (bf16[2,88,128]{2,1,0:T(8,128)(2,1)}, bf16[2,88,128]{2,1,0:T(8,128)(2,1)S(1)}, u32[]{:S(2)}, u32[]{:S(2)}) collective-permute-start(bf16[2,88,128]{2,1,0:T(8,128)(2,1)} %bitcast.174), channel_id=1, source_target_pairs={{0,0},{1,4},{2,8},{3,12},{4,16},{5,20},{6,24},{7,28},{8,1},{9,5},{... | collective-permute-start | bytes 135176 | tf_op jit(solution)/shard_map/ppermute | solution.py:1220
  18.6 13.0 %collective-permute-start.20 = (bf16[88,128]{1,0:T(8,128)(2,1)}, bf16[88,128]{1,0:T(8,128)(2,1)S(1)}, u32[]{:S(2)}, u32[]{:S(2)}) collective-permute-start(bf16[88,128]{1,0:T(8,128)(2,1)} %param.42), channel_id=1, source_target_pairs={{0,0},{1,4},{2,8},{3,12},{4,16},{5,20},{6,24},{7,28},{8,1},{9,5},{... | collective-permute-start | bytes 67592 | tf_op jit(solution)/shard_map/ppermute | solution.py:1220
  24.9 6.6 %collective-permute-start.18 = (bf16[32,128]{1,0:T(8,128)(2,1)S(1)}, bf16[32,128]{1,0:T(8,128)(2,1)S(1)}, u32[]{:S(2)}, u32[]{:S(2)}) collective-permute-start(bf16[32,128]{1,0:T(8,128)(2,1)S(1)} %collective-permute-done.17), channel_id=1, source_target_pairs={{0,2},{1,3},{2,0},{3,1},{4,6},{5,7},{6,4},{7,5},{8,10},{9,11},{10,... | collective-permute-start | bytes 24584 | tf_op jit(solution)/shard_map/ppermute | solution.py:1066
  30.7 114.7 %copy-start.69 = (s32[24]{0:T(128)S(1)}, s32[24]{0:T(128)}, u32[]{:S(2)}) copy-start(s32[24]{0:T(128)} %param.33) | copy-start | bytes 292
  30.8 117.2 %copy-start.54 = (bf16[1088,128]{1,0:T(8,128)(2,1)}, bf16[1088,128]{1,0:T(8,128)(2,1)S(1)}, u32[]{:S(2)}) copy-start(bf16[1088,128]{1,0:T(8,128)(2,1)S(1)} %constant_dynamic-update-slice_fusion.refs_4_) | copy-start | bytes 835588
  30.8 8.5 %collective-permute-start.9 = (bf16[1088,128]{1,0:T(8,128)(2,1)S(1)}, bf16[1088,128]{1,0:T(8,128)(2,1)S(1)}, u32[]{:S(2)}, u32[]{:S(2)}) collective-permute-start(bf16[1088,128]{1,0:T(8,128)(2,1)S(1)} %constant_dynamic-update-slice_fusion.refs_4_), channel_id=1, source_target_pairs={{0,24},{4,28},{8,16},{12,20},{16,8},{20,12},{24,0},{28,4},{1,25},{... | collective-permute-start | bytes 835592 | tf_op jit(solution)/shard_map/ppermute | solution.py:1071
  39.3 116.3 %copy-start.70 = (f32[8]{0:T(128)S(1)}, f32[8]{0:T(128)}, u32[]{:S(2)}) copy-start(f32[8]{0:T(128)} %param.31) | copy-start | bytes 100
  39.3 116.5 %copy-start.44 = (f32[1024]{0:T(1024)S(1)}, f32[1024]{0:T(1024)}, u32[]{:S(2)}) copy-start(f32[1024]{0:T(1024)} %param.24) | copy-start | bytes 12292
  39.3 70.8 %all-to-all-start = ((bf16[8,64,1024]{2,1,0:T(8,128)(2,1)}), bf16[8,64,1024]{2,1,0:T(8,128)(2,1)S(1)}, u32[]{:S(2)}, u32[]{:S(2)}) async-start(bf16[8,64,1024]{2,1,0:T(8,128)(2,1)} %bitcast.2), calls=%async_computation | async-start | bytes 2097152 | tf_op jit(solution)/shard_map/all_to_all | solution.py:1108
  46.0 44.5 %collective-permute-start.5 = (bf16[1088,128]{1,0:T(8,128)(2,1)S(1)}, bf16[1088,128]{1,0:T(8,128)(2,1)S(1)}, u32[]{:S(2)}, u32[]{:S(2)}) collective-permute-start(bf16[1088,128]{1,0:T(8,128)(2,1)S(1)} %constant_dynamic-update-slice_fusion.refs_4_), channel_id=1, source_target_pairs={{0,8},{4,12},{8,0},{12,4},{16,24},{20,28},{24,16},{28,20},{1,9},{5... | collective-permute-start | bytes 835592 | tf_op jit(solution)/shard_map/ppermute | solution.py:1071
  47.5 61.1 %collective-permute-start.7 = (bf16[1088,128]{1,0:T(8,128)(2,1)S(1)}, bf16[1088,128]{1,0:T(8,128)(2,1)S(1)}, u32[]{:S(2)}, u32[]{:S(2)}) collective-permute-start(bf16[1088,128]{1,0:T(8,128)(2,1)S(1)} %constant_dynamic-update-slice_fusion.refs_4_), channel_id=1, source_target_pairs={{0,16},{4,20},{8,24},{12,28},{16,0},{20,4},{24,8},{28,12},{1,17},{... | collective-permute-start | bytes 835592 | tf_op jit(solution)/shard_map/ppermute | solution.py:1071
  49.8 59.5 %collective-permute-start.4 = (bf16[1088,128]{1,0:T(8,128)(2,1)S(1)}, bf16[1088,128]{1,0:T(8,128)(2,1)S(1)}, u32[]{:S(2)}, u32[]{:S(2)}) collective-permute-start(bf16[1088,128]{1,0:T(8,128)(2,1)S(1)} %constant_dynamic-update-slice_fusion.refs_4_), channel_id=1, source_target_pairs={{0,4},{4,0},{8,12},{12,8},{16,20},{20,16},{24,28},{28,24},{1,5},{5... | collective-permute-start | bytes 835592 | tf_op jit(solution)/shard_map/ppermute | solution.py:1071
  50.4 74.0 %collective-permute-start.10 = (bf16[1088,128]{1,0:T(8,128)(2,1)S(1)}, bf16[1088,128]{1,0:T(8,128)(2,1)S(1)}, u32[]{:S(2)}, u32[]{:S(2)}) collective-permute-start(bf16[1088,128]{1,0:T(8,128)(2,1)S(1)} %collective-permute-done.9.refs_10_), channel_id=1, source_target_pairs={{0,4},{4,0},{8,12},{12,8},{16,20},{20,16},{24,28},{28,24},{1,5},{5... | collective-permute-start | bytes 835592 | tf_op jit(solution)/shard_map/ppermute | solution.py:1071
  90.5 18.8 %collective-permute-start.6 = (bf16[1088,128]{1,0:T(8,128)(2,1)S(1)}, bf16[1088,128]{1,0:T(8,128)(2,1)S(1)}, u32[]{:S(2)}, u32[]{:S(2)}) collective-permute-start(bf16[1088,128]{1,0:T(8,128)(2,1)S(1)} %collective-permute-done.5.refs_6_), channel_id=1, source_target_pairs={{0,4},{4,0},{8,12},{12,8},{16,20},{20,16},{24,28},{28,24},{1,5},{5... | collective-permute-start | bytes 835592 | tf_op jit(solution)/shard_map/ppermute | solution.py:1071
  108.6 15.0 %collective-permute-start.8 = (bf16[1088,128]{1,0:T(8,128)(2,1)S(1)}, bf16[1088,128]{1,0:T(8,128)(2,1)}, u32[]{:S(2)}, u32[]{:S(2)}) collective-permute-start(bf16[1088,128]{1,0:T(8,128)(2,1)S(1)} %collective-permute-done.7.refs_8_), channel_id=1, source_target_pairs={{0,4},{4,0},{8,12},{12,8},{16,20},{20,16},{24,28},{28,24},{1,5},{5... | collective-permute-start | bytes 835592 | tf_op jit(solution)/shard_map/ppermute | solution.py:1071
  110.2 26.2 %collective-permute-start.1 = (bf16[512,1024]{1,0:T(8,128)(2,1)S(1)}, bf16[512,1024]{1,0:T(8,128)(2,1)}, u32[]{:S(2)}, u32[]{:S(2)}) collective-permute-start(bf16[512,1024]{1,0:T(8,128)(2,1)S(1)} %bitcast.127), channel_id=1, source_target_pairs={{0,2},{1,3},{2,0},{3,1},{4,6},{5,7},{6,4},{7,5},{8,10},{9,11},{10,... | collective-permute-start | bytes 3145736 | tf_op jit(solution)/shard_map/ppermute | solution.py:1066
  124.5 20.3 %collective-permute-start.12 = (bf16[8,224,128]{2,1,0:T(8,128)(2,1)S(1)}, bf16[8,224,128]{2,1,0:T(8,128)(2,1)S(1)}, u32[]{:S(2)}, u32[]{:S(2)}) collective-permute-start(bf16[8,224,128]{2,1,0:T(8,128)(2,1)S(1)} %constant_dynamic-update-slice_fusion.6.refs_12_.f0), channel_id=1, source_target_pairs={{0,2},{1,3},{2,0},{3,1},{4,6},{5,7},{6,4},{7,5},{8,10},{9,11},{10,... | collective-permute-start | bytes 1376264 | tf_op jit(solution)/shard_map/ppermute | solution.py:1066
  124.9 30.8 %collective-permute-start = (bf16[512,1024]{1,0:T(8,128)(2,1)S(1)}, bf16[512,1024]{1,0:T(8,128)(2,1)}, u32[]{:S(2)}, u32[]{:S(2)}) collective-permute-start(bf16[512,1024]{1,0:T(8,128)(2,1)S(1)} %bitcast.128), channel_id=1, source_target_pairs={{0,1},{1,0},{2,3},{3,2},{4,5},{5,4},{6,7},{7,6},{8,9},{9,8},{10,11... | collective-permute-start | bytes 3145736 | tf_op jit(solution)/shard_map/ppermute | solution.py:1066
  136.4 19.3 %collective-permute-start.2 = (bf16[512,1024]{1,0:T(8,128)(2,1)}, bf16[512,1024]{1,0:T(8,128)(2,1)}, u32[]{:S(2)}, u32[]{:S(2)}) collective-permute-start(bf16[512,1024]{1,0:T(8,128)(2,1)} %collective-permute-done.1.refs_2_), channel_id=1, source_target_pairs={{0,1},{1,0},{2,3},{3,2},{4,5},{5,4},{6,7},{7,6},{8,9},{9,8},{10,11... | collective-permute-start | bytes 3145736 | tf_op jit(solution)/shard_map/ppermute | solution.py:1066
  144.8 2.4 collective-permute-start.13
  144.8 11.0 %collective-permute-start.11 = (bf16[8,224,128]{2,1,0:T(8,128)(2,1)S(1)}, bf16[8,224,128]{2,1,0:T(8,128)(2,1)}, u32[]{:S(2)}, u32[]{:S(2)}) collective-permute-start(bf16[8,224,128]{2,1,0:T(8,128)(2,1)S(1)} %constant_dynamic-update-slice_fusion.6.refs_12_.f0), channel_id=1, source_target_pairs={{0,1},{1,0},{2,3},{3,2},{4,5},{5,4},{6,7},{7,6},{8,9},{9,8},{10,11... | collective-permute-start | bytes 1376264 | tf_op jit(solution)/shard_map/ppermute | solution.py:1066
  148.0 52.3 %all-to-all-start.1 = ((bf16[8,64,1024]{2,1,0:T(8,128)(2,1)}), bf16[8,64,1024]{2,1,0:T(8,128)(2,1)S(1)}, u32[]{:S(2)}, u32[]{:S(2)}) async-start(bf16[8,64,1024]{2,1,0:T(8,128)(2,1)} %bitcast.147), calls=%async_computation.1 | async-start | bytes 2097152 | tf_op jit(solution)/shard_map/all_to_all | solution.py:1108
  152.8 274.1 %reduce-scatter.4.cloned.1.call-start = ((), (), s32[]{:S(2)}) async-start(), calls=%async_computation.6 | async-start | bytes 2985984
  199.4 14.0 %collective-permute-start.14 = (bf16[1024,256]{1,0:T(8,128)(2,1)}, bf16[1024,256]{1,0:T(8,128)(2,1)S(1)}, u32[]{:S(2)}, u32[]{:S(2)}) collective-permute-start(bf16[1024,256]{1,0:T(8,128)(2,1)} %get-tuple-element.105), channel_id=1, source_target_pairs={{0,2},{1,3},{2,0},{3,1},{4,6},{5,7},{6,4},{7,5},{8,10},{9,11},{10,... | collective-permute-start | bytes 1572872 | tf_op jit(solution)/shard_map/ppermute | solution.py:1066
  213.4 24.2 %collective-permute-start.15 = (bf16[512,1024]{1,0:T(8,128)(2,1)S(1)}, bf16[512,1024]{1,0:T(8,128)(2,1)}, u32[]{:S(2)}, u32[]{:S(2)}) collective-permute-start(bf16[512,1024]{1,0:T(8,128)(2,1)S(1)} %bitcast.134), channel_id=1, source_target_pairs={{0,2},{1,3},{2,0},{3,1},{4,6},{5,7},{6,4},{7,5},{8,10},{9,11},{10,... | collective-permute-start | bytes 3145736 | tf_op jit(solution)/shard_map/ppermute | solution.py:1066
  249.2 2.7 collective-permute-start.21
  249.2 4.4 collective-permute-start.23
  252.6 2.7 collective-permute-start.22
  252.8 25.4 %collective-permute-start.25 = (bf16[512,1024]{1,0:T(8,128)(2,1)S(1)}, bf16[512,1024]{1,0:T(8,128)(2,1)S(1)}, u32[]{:S(2)}, u32[]{:S(2)}) collective-permute-start(bf16[512,1024]{1,0:T(8,128)(2,1)S(1)} %get-tuple-element.119.x0.refs_0_), channel_id=1, source_target_pairs={{0,2},{1,3},{2,0},{3,1},{4,6},{5,7},{6,4},{7,5},{8,10},{9,11},{10,... | collective-permute-start | bytes 3145736 | tf_op jit(solution)/shard_map/ppermute | solution.py:1066
  253.6 24.7 %collective-permute-start.27 = (bf16[512,1024]{1,0:T(8,128)(2,1)}, bf16[512,1024]{1,0:T(8,128)(2,1)S(1)}, u32[]{:S(2)}, u32[]{:S(2)}) collective-permute-start(bf16[512,1024]{1,0:T(8,128)(2,1)} %collective-permute-done.15.g0.refs_6_), channel_id=1, source_target_pairs={{0,1},{1,0},{2,3},{3,2},{4,5},{5,4},{6,7},{7,6},{8,9},{9,8},{10,11... | collective-permute-start | bytes 3145736 | tf_op jit(solution)/shard_map/ppermute | solution.py:1066
  278.3 2.7 collective-permute-start.26
  298.9 2.7 collective-permute-start.28
  302.0 25.3 %collective-permute-start.29 = (bf16[512,1024]{1,0:T(8,128)(2,1)S(1)}, bf16[512,1024]{1,0:T(8,128)(2,1)S(1)}, u32[]{:S(2)}, u32[]{:S(2)}) collective-permute-start(bf16[512,1024]{1,0:T(8,128)(2,1)S(1)} %add_convert_fusion.3), channel_id=1, source_target_pairs={{0,2},{1,3},{2,0},{3,1},{4,6},{5,7},{6,4},{7,5},{8,10},{9,11},{10,... | collective-permute-start | bytes 3145736 | tf_op jit(solution)/shard_map/ppermute | solution.py:1066
  302.8 24.5 %collective-permute-start.24 = (bf16[512,1024]{1,0:T(8,128)(2,1)S(1)}, bf16[512,1024]{1,0:T(8,128)(2,1)S(1)}, u32[]{:S(2)}, u32[]{:S(2)}) collective-permute-start(bf16[512,1024]{1,0:T(8,128)(2,1)S(1)} %get-tuple-element.125), channel_id=1, source_target_pairs={{0,1},{1,0},{2,3},{3,2},{4,5},{5,4},{6,7},{7,6},{8,9},{9,8},{10,11... | collective-permute-start | bytes 3145736 | tf_op jit(solution)/shard_map/ppermute | solution.py:1066
  328.9 3.6 collective-permute-start.30
  329.0 12.6 %collective-permute-start.32 = (bf16[512,1024]{1,0:T(8,128)(2,1)}, bf16[512,1024]{1,0:T(8,128)(2,1)}, u32[]{:S(2)}, u32[]{:S(2)}) collective-permute-start(bf16[512,1024]{1,0:T(8,128)(2,1)} %get-tuple-element.154), channel_id=1, source_target_pairs={{0,1},{1,0},{2,3},{3,2},{4,5},{5,4},{6,7},{7,6},{8,9},{9,8},{10,11... | collective-permute-start | bytes 3145736 | tf_op jit(solution)/shard_map/ppermute | solution.py:1066
  337.2 14.0 %collective-permute-start.31 = (bf16[1024,256]{1,0:T(8,128)(2,1)S(1)}, bf16[1024,256]{1,0:T(8,128)(2,1)S(1)}, u32[]{:S(2)}, u32[]{:S(2)}) collective-permute-start(bf16[1024,256]{1,0:T(8,128)(2,1)S(1)} %get-tuple-element.152), channel_id=1, source_target_pairs={{0,2},{1,3},{2,0},{3,1},{4,6},{5,7},{6,4},{7,5},{8,10},{9,11},{10,... | collective-permute-start | bytes 1572872 | tf_op jit(solution)/shard_map/ppermute | solution.py:1066
  351.3 30.6 %collective-permute-start.33 = (bf16[512,1024]{1,0:T(8,128)(2,1)S(1)}, bf16[512,1024]{1,0:T(8,128)(2,1)S(1)}, u32[]{:S(2)}, u32[]{:S(2)}) collective-permute-start(bf16[512,1024]{1,0:T(8,128)(2,1)S(1)} %add_convert_fusion.2), channel_id=1, source_target_pairs={{0,2},{1,3},{2,0},{3,1},{4,6},{5,7},{6,4},{7,5},{8,10},{9,11},{10,... | collective-permute-start | bytes 3145736 | tf_op jit(solution)/shard_map/ppermute | solution.py:1066
  352.0 34.3 %collective-permute-start.36 = (bf16[512,1024]{1,0:T(8,128)(2,1)S(1)}, bf16[512,1024]{1,0:T(8,128)(2,1)S(1)}, u32[]{:S(2)}, u32[]{:S(2)}) collective-permute-start(bf16[512,1024]{1,0:T(8,128)(2,1)S(1)} %copy-done.48), channel_id=1, source_target_pairs={{0,1},{1,0},{2,3},{3,2},{4,5},{5,4},{6,7},{7,6},{8,9},{9,8},{10,11... | collective-permute-start | bytes 3145736 | tf_op jit(solution)/shard_map/ppermute | solution.py:1066
  385.7 2.8 collective-permute-start.34
  390.0 32.1 %all-to-all-start.2 = ((bf16[8,64,1024]{2,1,0:T(8,128)(2,1)}), bf16[8,64,1024]{2,1,0:T(8,128)(2,1)}, u32[]{:S(2)}, u32[]{:S(2)}) async-start(bf16[8,64,1024]{2,1,0:T(8,128)(2,1)} %bitcast.144), calls=%async_computation.2 | async-start | bytes 2097152 | tf_op jit(solution)/shard_map/all_to_all | solution.py:1108
  396.0 25.2 %collective-permute-start.35 = (bf16[512,1024]{1,0:T(8,128)(2,1)}, bf16[512,1024]{1,0:T(8,128)(2,1)}, u32[]{:S(2)}, u32[]{:S(2)}) collective-permute-start(bf16[512,1024]{1,0:T(8,128)(2,1)} %add_convert_fusion.1), channel_id=1, source_target_pairs={{0,2},{1,3},{2,0},{3,1},{4,6},{5,7},{6,4},{7,5},{8,10},{9,11},{10,... | collective-permute-start | bytes 3145736 | tf_op jit(solution)/shard_map/ppermute | solution.py:1066
  405.7 16.4 %collective-permute-start.37 = (bf16[512,1024]{1,0:T(8,128)(2,1)}, bf16[512,1024]{1,0:T(8,128)(2,1)}, u32[]{:S(2)}, u32[]{:S(2)}) collective-permute-start(bf16[512,1024]{1,0:T(8,128)(2,1)} %get-tuple-element.179), channel_id=1, source_target_pairs={{0,1},{1,0},{2,3},{3,2},{4,5},{5,4},{6,7},{7,6},{8,9},{9,8},{10,11... | collective-permute-start | bytes 3145736 | tf_op jit(solution)/shard_map/ppermute | solution.py:1066
  428.7 60.1 %all-to-all-start.3 = ((bf16[8,64,1024]{2,1,0:T(8,128)(2,1)}), bf16[8,64,1024]{2,1,0:T(8,128)(2,1)S(1)}, u32[]{:S(2)}, u32[]{:S(2)}) async-start(bf16[8,64,1024]{2,1,0:T(8,128)(2,1)} %bitcast.34), calls=%async_computation.3 | async-start | bytes 2097152 | tf_op jit(solution)/shard_map/all_to_all | solution.py:1108
  434.0 5.1 %collective-permute-start.39 = (bf16[256,512]{1,0:T(8,128)(2,1)S(1)}, bf16[256,512]{1,0:T(8,128)(2,1)S(1)}, u32[]{:S(2)}, u32[]{:S(2)}) collective-permute-start(bf16[256,512]{1,0:T(8,128)(2,1)S(1)} %get-tuple-element.197), channel_id=1, source_target_pairs={{0,1},{1,0},{2,3},{3,2},{4,5},{5,4},{6,7},{7,6},{8,9},{9,8},{10,11... | collective-permute-start | bytes 786440 | tf_op jit(solution)/shard_map/ppermute | solution.py:1066
  434.1 13.1 %collective-permute-start.38 = (bf16[256,512]{1,0:T(8,128)(2,1)S(1)}, bf16[256,512]{1,0:T(8,128)(2,1)S(1)}, u32[]{:S(2)}, u32[]{:S(2)}) collective-permute-start(bf16[256,512]{1,0:T(8,128)(2,1)S(1)} %get-tuple-element.196), channel_id=1, source_target_pairs={{0,1},{1,0},{2,3},{3,2},{4,5},{5,4},{6,7},{7,6},{8,9},{9,8},{10,11... | collective-permute-start | bytes 786440 | tf_op jit(solution)/shard_map/ppermute | solution.py:1066
  434.7 1.7 collective-permute-start.51
  434.8 17.5 %collective-permute-start.41 = (bf16[8,32,128]{2,1,0:T(8,128)(2,1)S(1)}, bf16[8,32,128]{2,1,0:T(8,128)(2,1)S(1)}, u32[]{:S(2)}, u32[]{:S(2)}) collective-permute-start(bf16[8,32,128]{2,1,0:T(8,128)(2,1)S(1)} %bitcast.166), channel_id=1, source_target_pairs={{0,2},{1,3},{2,0},{3,1},{4,6},{5,7},{6,4},{7,5},{8,10},{9,11},{10,... | collective-permute-start | bytes 196616 | tf_op jit(solution)/shard_map/ppermute | solution.py:1066
  436.2 6.8 %collective-permute-start.50 = (f32[96,128]{1,0:T(8,128)S(1)}, f32[96,128]{1,0:T(8,128)S(1)}, u32[]{:S(2)}, u32[]{:S(2)}) collective-permute-start(f32[96,128]{1,0:T(8,128)S(1)} %get-tuple-element.205), channel_id=1, source_target_pairs={{0,1},{1,0},{2,3},{3,2},{4,5},{5,4},{6,7},{7,6},{8,9},{9,8},{10,11... | collective-permute-start | bytes 147464 | tf_op jit(solution)/shard_map/ppermute | solution.py:1066
  436.4 32.3 %collective-permute-start.53 = (f32[264,128]{1,0:T(8,128)S(1)}, f32[264,128]{1,0:T(8,128)S(1)}, u32[]{:S(2)}, u32[]{:S(2)}) collective-permute-start(f32[264,128]{1,0:T(8,128)S(1)} %slice.163), channel_id=1, source_target_pairs={{0,0},{4,1},{8,2},{12,3},{16,4},{20,5},{24,6},{28,7},{1,8},{5,9},{... | collective-permute-start | bytes 405512 | tf_op jit(solution)/shard_map/ppermute | solution.py:1386
  439.1 6.1 %collective-permute-start.52 = (f32[96,128]{1,0:T(8,128)S(1)}, f32[96,128]{1,0:T(8,128)S(1)}, u32[]{:S(2)}, u32[]{:S(2)}) collective-permute-start(f32[96,128]{1,0:T(8,128)S(1)} %slice_add_fusion), channel_id=1, source_target_pairs={{0,2},{1,3},{2,0},{3,1},{4,6},{5,7},{6,4},{7,5},{8,10},{9,11},{10,... | collective-permute-start | bytes 147464 | tf_op jit(solution)/shard_map/ppermute | solution.py:1066
  443.0 9.0 %collective-permute-start.40 = (bf16[256,512]{1,0:T(8,128)(2,1)S(1)}, bf16[256,512]{1,0:T(8,128)(2,1)S(1)}, u32[]{:S(2)}, u32[]{:S(2)}) collective-permute-start(bf16[256,512]{1,0:T(8,128)(2,1)S(1)} %fusion), channel_id=1, source_target_pairs={{0,2},{1,3},{2,0},{3,1},{4,6},{5,7},{6,4},{7,5},{8,10},{9,11},{10,... | collective-permute-start | bytes 786440 | tf_op jit(solution)/shard_map/ppermute | solution.py:1066
  452.4 18.3 %collective-permute-start.48 = (bf16[256,128]{1,0:T(8,128)(2,1)S(1)}, bf16[256,128]{1,0:T(8,128)(2,1)S(1)}, u32[]{:S(2)}, u32[]{:S(2)}) collective-permute-start(bf16[256,128]{1,0:T(8,128)(2,1)S(1)} %get-tuple-element.199), channel_id=1, source_target_pairs={{0,28},{4,24},{8,20},{12,16},{16,12},{20,8},{24,4},{28,0},{1,29},{... | collective-permute-start | bytes 196616 | tf_op jit(solution)/shard_map/ppermute | solution.py:1071
  454.4 20.9 %collective-permute-start.47 = (bf16[256,128]{1,0:T(8,128)(2,1)S(1)}, bf16[256,128]{1,0:T(8,128)(2,1)S(1)}, u32[]{:S(2)}, u32[]{:S(2)}) collective-permute-start(bf16[256,128]{1,0:T(8,128)(2,1)S(1)} %get-tuple-element.200), channel_id=1, source_target_pairs={{0,24},{4,28},{8,16},{12,20},{16,8},{20,12},{24,0},{28,4},{1,25},{... | collective-permute-start | bytes 196616 | tf_op jit(solution)/shard_map/ppermute | solution.py:1071
  469.4 6.9 %collective-permute-start.46 = (bf16[256,128]{1,0:T(8,128)(2,1)S(1)}, bf16[256,128]{1,0:T(8,128)(2,1)S(1)}, u32[]{:S(2)}, u32[]{:S(2)}) collective-permute-start(bf16[256,128]{1,0:T(8,128)(2,1)S(1)} %get-tuple-element.201), channel_id=1, source_target_pairs={{0,20},{4,16},{8,28},{12,24},{16,4},{20,0},{24,12},{28,8},{1,21},{... | collective-permute-start | bytes 196616 | tf_op jit(solution)/shard_map/ppermute | solution.py:1071
  469.4 6.9 %collective-permute-start.45 = (bf16[256,128]{1,0:T(8,128)(2,1)S(1)}, bf16[256,128]{1,0:T(8,128)(2,1)S(1)}, u32[]{:S(2)}, u32[]{:S(2)}) collective-permute-start(bf16[256,128]{1,0:T(8,128)(2,1)S(1)} %get-tuple-element.202), channel_id=1, source_target_pairs={{0,16},{4,20},{8,24},{12,28},{16,0},{20,4},{24,8},{28,12},{1,17},{... | collective-permute-start | bytes 196616 | tf_op jit(solution)/shard_map/ppermute | solution.py:1071
  469.7 8.3 %collective-permute-start.44 = (bf16[256,128]{1,0:T(8,128)(2,1)S(1)}, bf16[256,128]{1,0:T(8,128)(2,1)S(1)}, u32[]{:S(2)}, u32[]{:S(2)}) collective-permute-start(bf16[256,128]{1,0:T(8,128)(2,1)S(1)} %get-tuple-element.203), channel_id=1, source_target_pairs={{0,12},{4,8},{8,4},{12,0},{16,28},{20,24},{24,20},{28,16},{1,13},{... | collective-permute-start | bytes 196616 | tf_op jit(solution)/shard_map/ppermute | solution.py:1071
  470.7 8.0 %collective-permute-start.43 = (bf16[256,128]{1,0:T(8,128)(2,1)S(1)}, bf16[256,128]{1,0:T(8,128)(2,1)S(1)}, u32[]{:S(2)}, u32[]{:S(2)}) collective-permute-start(bf16[256,128]{1,0:T(8,128)(2,1)S(1)} %get-tuple-element.204), channel_id=1, source_target_pairs={{0,8},{4,12},{8,0},{12,4},{16,24},{20,28},{24,16},{28,20},{1,9},{5... | collective-permute-start | bytes 196616 | tf_op jit(solution)/shard_map/ppermute | solution.py:1071
  475.2 4.3 collective-permute-start.42
  479.6 8.0 %collective-permute-start.49 = (f32[128,128]{1,0:T(8,128)S(1)}, f32[128,128]{1,0:T(8,128)S(1)}, u32[]{:S(2)}, u32[]{:S(2)}) collective-permute-start(f32[128,128]{1,0:T(8,128)S(1)} %slice.184), channel_id=1, source_target_pairs={{0,0},{4,1},{8,2},{12,3},{16,4},{20,5},{24,6},{28,7},{1,8},{5,9},{... | collective-permute-start | bytes 196616 | tf_op jit(solution)/shard_map/ppermute | solution.py:1314
  (67 other events, 1318.2 us)
Sparse Core Ops, SparseCore 0:
  39.4 139.9 all-gather.2
  329.6 71.0 reduce-scatter.3
